TPU v7x, 256 devices: a whole 4x4x8 slice. The times are simulated.
256 devices in a mesh: proto: 64 (over x, z, core), crop: 4 (over y).
Axes of the slice: x: 4, y: 4, z: 8, core: 2. Of those that a mesh axis runs over, the one named last changes fastest.
Arguments:
- teacher_feats: float32 [384, 2048], P('proto', 'crop'), may hold values from -4 to 4
- student_feats: float32 [384, 2048], P('proto', 'crop'), may hold values from -4 to 4
- prototypes: float32 [384, 131072], P(None, 'proto'), may hold values from -4 to 4
Outputs:
- grad_features: float32 [384, 2048], P('proto', 'crop')
- grad_protos: float32 [384, 131072], P('crop', 'proto')
- loss: float32 [], replicated
All inputs are finite; a program needn't handle non-finite values.
Results may differ from a plain program's by a relative error of at most 0.0003.
Values sent between devices are 32-bit elements; how exact they have to be, the bound alone decides.
A program may use at most 64 MiB of HBM per device.

v0:
```python
import math

import jax
import jax.numpy as jnp
from jax import lax
from jax.sharding import PartitionSpec as P

ITERS = 3


teacher_temp = 0.07
student_temp = 0.1
norm_eps = 1e-06
highest = lax.Precision.HIGHEST


def unit_columns(matrix):
    return matrix / jnp.sqrt(jnp.sum(matrix * matrix, axis=0, keepdims=True) + norm_eps)


def project(columns, weights):
    return lax.dot_general(
        columns,
        weights,
        (((0,), (0,)), ((), ())),
        precision=highest,
        preferred_element_type=jnp.float32,
    )


def column_total(values, crop_scale):
    return lax.psum(jnp.sum(values * crop_scale[:, None], axis=0), "crop")


def row_total(values, scaling):
    return lax.psum(jnp.sum(values * scaling[None, :], axis=1), "proto")


def on_device(teacher_feats, student_feats, prototypes):
    full_teacher, full_student = (
        lax.all_gather(teacher_feats, "proto", axis=0, tiled=True),
        lax.all_gather(student_feats, "proto", axis=0, tiled=True),
    )
    weights = unit_columns(prototypes)
    teacher = unit_columns(full_teacher)
    student = unit_columns(full_student)
    local_crops = teacher.shape[1]
    width = weights.shape[0]
    crop_count = local_crops * lax.axis_size("crop")
    scale = math.sqrt(weights.shape[1] * lax.axis_size("proto"))
    values = jnp.exp(project(teacher, weights) / teacher_temp)
    logits = project(student, weights) / student_temp
    student_exp = jnp.exp(logits)
    crop_scale = jnp.ones((local_crops,), jnp.float32)
    scaling = 1.0 / column_total(values, crop_scale)
    for step in range(ITERS - 1):
        crop_scale = 1.0 / row_total(values, scaling)
        scaling = 1.0 / column_total(values, crop_scale)
    weighted = values * scaling[None, :]
    last_rows = lax.psum(jnp.sum(weighted, axis=1), "proto")
    crop_scale = 1.0 / last_rows
    targets = weighted * crop_scale[:, None]
    student_total = lax.psum(jnp.sum(student_exp, axis=1), "proto")
    lse = jnp.log(student_total)
    share = jnp.sum(lse) / lax.axis_size("proto") - jnp.sum(targets * logits)
    loss_sum = lax.psum(share, ("proto", "crop"))
    probs = jnp.exp(logits - lse[:, None])
    grads = (probs - targets) * (scale / student_temp)
    feat_rows = width // lax.axis_size("proto")
    whole = lax.dot_general(
        weights,
        grads,
        (((1,), (1,)), ((), ())),
        precision=highest,
        preferred_element_type=jnp.float32,
    )
    summed = lax.psum(whole, "proto")
    grad_features = lax.dynamic_slice_in_dim(
        summed, lax.axis_index("proto") * feat_rows, feat_rows, 0
    )
    grad_protos = lax.psum_scatter(
        jnp.dot(student, grads, precision=highest, preferred_element_type=jnp.float32),
        "crop",
        scatter_dimension=0,
        tiled=True,
    )
    return (grad_features, grad_protos, loss_sum / crop_count)


def solution(mesh):
    placed = (P("proto", "crop"), P("proto", "crop"), P(None, "proto"))
    return jax.shard_map(
        on_device,
        mesh=mesh,
        in_specs=placed,
        out_specs=(P("proto", "crop"), P("crop", "proto"), P()),
        check_vma=False,
    )
```

profile of v0, /device:TPU:1, one launch (start us, length us, event | category | flops | bytes accessed | tf_op | source)
XLA Modules:
  0.0 871.2 jit_solution(6473876252542923696)
XLA Ops:
  8.0 2.2 multiply_reduce_fusion.6
  10.2 54.9 %all-gather.1 = f32[64,6,512]{2,1,0:T(8,128)S(1)} all-gather(f32[1,6,512]{2,1,0:T(8,128)} %bitcast.2), channel_id=1, replica_groups=mesh['proto'=64,'crop'=4] {'proto'}, dimensions={0}, use_global_device_ids=true | all-gather | bytes 798720 | tf_op jit(solution)/shard_map/all_gather | solution.py:41
  65.3 10.0 %fusion.5 = (f32[2048]{0:T(1024)S(1)}, f32[512,2048]{1,0:T(8,128)}) fusion(f32[384,2048]{1,0:T(8,128)} %param.5, f32[2048]{0:T(1024)S(1)} %add_sqrt_fusion, f32[384,512]{1,0:T(8,128)S(1)} %reshape.34, f32[512]{0:T(512)S(1)} %add_sqrt_fusion.1), kind=kOutput, calls=%fused_computation.30 | convolution fusion | flops 4834916352 | bytes 8144896 | tf_op jit(solution)/shard_map/dot_general | solution.py:22
  75.3 8.8 %psum.64 = f32[2048]{0:T(1024)S(1)} all-reduce(f32[2048]{0:T(1024)S(1)} %get-tuple-element.7), channel_id=1, replica_groups=mesh['proto'=64,'crop'=4] {'crop'}, use_global_device_ids=true, to_apply=%region_6.0 | all-reduce | flops 2048 | bytes 16384 | tf_op jit(solution)/shard_map/psum | solution.py:32
  84.1 2.6 multiply_reduce_fusion.4
  86.6 125.6 %psum.65 = f32[512]{0:T(512)S(1)} all-reduce(f32[512]{0:T(512)S(1)} %multiply_reduce_fusion.4), channel_id=1, replica_groups=mesh['proto'=64,'crop'=4] {'proto'}, use_global_device_ids=true, to_apply=%region_8.0 | all-reduce | flops 512 | bytes 4096 | tf_op jit(solution)/shard_map/psum | solution.py:36
  212.2 2.5 multiply_reduce_fusion.3
  214.8 6.1 psum.66
  220.9 2.6 multiply_reduce_fusion.2
  223.5 126.4 %psum.67 = f32[512]{0:T(512)S(1)} all-reduce(f32[512]{0:T(512)S(1)} %multiply_reduce_fusion.2), channel_id=1, replica_groups=mesh['proto'=64,'crop'=4] {'proto'}, use_global_device_ids=true, to_apply=%region_12.0 | all-reduce | flops 512 | bytes 4096 | tf_op jit(solution)/shard_map/psum | solution.py:36
  349.9 2.6 multiply_reduce_fusion.1
  352.5 7.8 psum.68
  360.3 2.6 multiply_reduce_fusion.5
  362.9 126.1 %psum.69 = f32[512]{0:T(512)S(1)} all-reduce(f32[512]{0:T(512)S(1)} %multiply_reduce_fusion.5), channel_id=1, replica_groups=mesh['proto'=64,'crop'=4] {'proto'}, use_global_device_ids=true, to_apply=%region_16.0 | all-reduce | flops 512 | bytes 4096 | tf_op jit(solution)/shard_map/psum | solution.py:60
  488.9 47.8 %all-gather = f32[64,6,512]{2,1,0:T(8,128)S(1)} all-gather(f32[1,6,512]{2,1,0:T(8,128)S(1)} %bitcast.3), channel_id=1, replica_groups=mesh['proto'=64,'crop'=4] {'proto'}, dimensions={0}, use_global_device_ids=true | all-gather | bytes 798720 | tf_op jit(solution)/shard_map/all_gather | solution.py:42
  537.0 12.0 %multiply_reduce_fusion = (f32[]{:T(128)}, f32[512]{0:T(512)S(1)}, f32[512,2048]{1,0:T(8,128)}) fusion(f32[512,2048]{1,0:T(8,128)} %get-tuple-element.8, f32[512]{0:T(512)S(1)} %broadcast_divide_fusion.7, f32[2048]{0:T(1024)S(1)} %broadcast_divide_fusion.4, f32[384,2048]{1,0:T(8,128)} %param.5, f32[2048]{0:T(1024)S(1)} %add_sqrt_fusion, ...), kind=kOutput, calls=%fused_computation | convolution fusion | flops 4839112192 | bytes 12343300 | tf_op jit(solution)/shard_map/dot_general | solution.py:22
  548.9 123.6 %psum.63 = f32[512]{0:T(512)S(1)} all-reduce(f32[512]{0:T(512)S(1)} %get-tuple-element.4), channel_id=1, replica_groups=mesh['proto'=64,'crop'=4] {'proto'}, use_global_device_ids=true, to_apply=%region_3.0 | all-reduce | flops 512 | bytes 4096 | tf_op jit(solution)/shard_map/psum | solution.py:63
  672.5 0.6 log_reduce_fusion
  673.1 10.6 %fusion.4 = f32[384,512]{1,0:T(8,128)} fusion(f32[384,2048]{1,0:T(8,128)} %param.5, f32[2048]{0:T(1024)S(1)} %add_sqrt_fusion, f32[512,2048]{1,0:T(8,128)} %get-tuple-element.8, f32[512,2048]{1,0:T(8,128)} %get-tuple-element.9, f32[512]{0:T(512)S(1)} %broadcast_divide_fusion.7, f32[2048]{0:T(1024)S(1)} %broadcast_divide_fusion.4, f32[512]{0:T(512)S(1)} %get-tuple-element.6), kind=kOutput, calls=%fused_computation.29 | convolution fusion | flops 4838916096 | bytes 12341248 | tf_op jit(solution)/shard_map/dot_general | solution.py:70
  683.7 0.3 reduce-scatter.2.cloned.1.call-start
  684.0 10.0 %fusion.2 = f32[384,2048]{1,0:T(8,128)} fusion(f32[384,512]{1,0:T(8,128)S(1)} %reshape.32, f32[512]{0:T(512)S(1)} %add_sqrt_fusion.2, f32[512,2048]{1,0:T(8,128)} %get-tuple-element.8, f32[512,2048]{1,0:T(8,128)} %get-tuple-element.9, f32[512]{0:T(512)S(1)} %broadcast_divide_fusion.7, f32[2048]{0:T(1024)S(1)} %broadcast_divide_fusion.4, ...), kind=kOutput, calls=%fused_computation.16 | convolution fusion | flops 4838326272 | bytes 12335104 | tf_op jit(solution)/shard_map/dot_general | solution.py:82
  695.4 75.3 %psum.71 = f32[]{:T(128)} all-reduce(f32[]{:T(128)S(6)} %sub.17), channel_id=1, replica_groups=mesh['proto'=64,'crop'=4] {'proto','crop'}, use_global_device_ids=true, to_apply=%region_21.0 | all-reduce | flops 1 | bytes 8 | tf_op jit(solution)/shard_map/psum | solution.py:66
  771.4 89.9 %all-reduce.2.cloned.1.call-done = f32[384,512]{1,0:T(8,128)} async-done(((f32[384,512]{1,0:T(8,128)}), f32[384,512]{1,0:T(8,128)}) %all-reduce.2.cloned.1.call-update) | async-done | bytes 786448 | tf_op jit(solution)/shard_map/psum | solution.py:77
  861.3 1.4 constant_dynamic-slice_fusion
  (19 shorter events, 0.5 us)
Async XLA Ops:
  8.0 853.3 %all-reduce.2.cloned.1.call-start = ((), (), s32[]{:S(2)}) async-start(), calls=%async_computation.1 | async-start | bytes 1572864 | tf_op jit(solution)/shard_map/psum | solution.py:77
  349.9 139.0 %copy-start = (f32[6,512]{1,0:T(8,128)S(1)}, f32[6,512]{1,0:T(8,128)}, u32[]{:S(2)}) copy-start(f32[6,512]{1,0:T(8,128)} %param.4) | copy-start | bytes 36868
  683.7 178.9 %reduce-scatter.2.cloned.1.call-start = ((), (), s32[]{:S(2)}) async-start(), calls=%async_computation.2 | async-start | bytes 3932160 | tf_op jit(solution)/shard_map/reduce_scatter | solution.py:81
Sparse Core Ops, SparseCore 0:
  683.9 177.3 all-reduce.1
Sparse Core Ops, SparseCore 1:
  694.2 35.9 reduce-scatter.1
where the time goes:
time: 873 us; the launch traced here: 871 us
  blocking collectives  702 us (80%)
  waiting for transfers between devices  89.9 us (10%)
  matrix products  42.6 us (5%)
  between operations  18.6 us (2%)
  other arithmetic  15.8 us (2%)
    psum x2, blocking collectives, row_total(): return lax.psum(jnp.sum(values * scaling[None, :], axis=1), 'proto')  252 us
    psum x1, blocking collectives, on_device(): last_rows = lax.psum(jnp.sum(weighted, axis=1), 'proto')  126 us
    psum x1, blocking collectives, on_device(): student_total = lax.psum(jnp.sum(student_exp, axis=1), 'proto')  124 us
    psum x1, waiting for transfers between devices, on_device(): summed = lax.psum(whole, 'proto')  89.9 us
    psum x1, blocking collectives, on_device(): loss_sum = lax.psum(share, ('proto', 'crop'))  75.3 us
    all_gather x1, blocking collectives, on_device(): lax.all_gather(teacher_feats, 'proto', axis=0, tiled=True)  54.9 us
    all_gather x1, blocking collectives, on_device(): lax.all_gather(student_feats, 'proto', axis=0, tiled=True)  47.8 us
    psum x3, blocking collectives, column_total(): return lax.psum(jnp.sum(values * crop_scale[:, None], axis=0), 'crop')  22.7 us
  transfers between devices with their start and end apart: 2, of which 1 were waited for; matrix products, arithmetic and copies ran while one was open for 1% of the time, Pallas kernels for 0%

commit v1 on v0

v1 whole, which is shorter than its diff:
```python
import functools
import math

import jax
import jax.numpy as jnp
from jax import lax
from jax.experimental import pallas as pl
from jax.experimental.pallas import tpu as pltpu
from jax.sharding import PartitionSpec as P

MESH = pl.DeviceIdType.MESH
TEACHER_TEMP = 0.07
STUDENT_TEMP = 0.1
EPS = 1e-06
ITERS = 3
f32 = jnp.float32
bf16 = jnp.bfloat16
LANES = 128


def split(x):
    hi = x.astype(bf16)
    return hi, (x - hi.astype(f32)).astype(bf16)


def await_bytes(ref, sem):
    pltpu.make_async_copy(ref, ref, sem).wait()


def nn(a, b):
    return lax.dot_general(a, b, (((1,), (0,)), ((), ())), preferred_element_type=f32)


def nt(a, b):
    return lax.dot_general(a, b, (((1,), (1,)), ((), ())), preferred_element_type=f32)


def kernel(
    n_y, n_chip, scale, crops_all,
    t_ref, s_ref, w_ref,
    gf_ref, gp_ref, loss_ref,
    gt, gs, flat, zt_cat, zs_cat, zs_hi, zs_lo, w_cat, e_ref, s_log, es_ref, g_hi, g_lo,
    tcol, vcol, col_out, col_in, ubuf, row_out, row_in, gf_acc, rs_flat, rs_src, rs_pair, rs_in,
    loss_in,
    sem_g_s, sem_g_r, sem_d_s, sem_d_r, sem_c_s, sem_c_r, sem_r_s, sem_r_r, sem_f_s, sem_f_r,
    sem_l_s, sem_l_r,
):
    p = lax.axis_index("proto")
    y = lax.axis_index("crop")
    chip = p // 2
    core = p % 2
    width, protos = w_ref.shape
    crops = e_ref.shape[0]
    n_ct = crops // LANES
    n_pt = protos // LANES
    feat = width // (2 * n_chip)
    n_plane = 2 * n_chip

    bar = pltpu.get_barrier_semaphore()

    def greet_plane(i, c):
        pl.semaphore_signal(bar, inc=1, device_id=(lax.rem(p + i, n_plane), y), device_id_type=MESH)
        return c

    lax.fori_loop(1, n_plane, greet_plane, 0)
    for i in range(1, n_y):
        pl.semaphore_signal(bar, inc=1, device_id=(p, lax.rem(y + i, n_y)), device_id_type=MESH)

    for src, dst in ((t_ref, gt), (s_ref, gs)):
        for j in range(feat):
            for ct in range(n_ct):
                k = n_ct * j + ct
                dst[chip, core, k : k + 1, :] = src[j : j + 1, ct * LANES : (ct + 1) * LANES]

    def prep_w(i, c):
        cols = pl.ds(pl.multiple_of(i * 256, 256), 256)
        w = w_ref[:, cols]
        w = w * (1.0 / jnp.sqrt(jnp.sum(w * w, axis=0, keepdims=True) + EPS))
        hi, lo = split(w)
        w_cat[0:width, cols] = hi
        w_cat[width : 2 * width, cols] = hi
        w_cat[2 * width : 3 * width, cols] = lo
        return c

    lax.fori_loop(0, protos // 256, prep_w, 0)
    pl.semaphore_wait(bar, n_plane - 1 + n_y - 1)

    def gather_start(buf, k):
        def go(i, c):
            other = lax.rem(chip + i, n_chip)
            pltpu.make_async_remote_copy(
                src_ref=buf.at[chip, core],
                dst_ref=buf.at[chip, core],
                send_sem=sem_g_s.at[k],
                recv_sem=sem_g_r.at[k],
                device_id=(other * 2 + core, y),
                device_id_type=MESH,
            ).start()
            return c

        lax.fori_loop(1, n_chip, go, 0)

    def gather_finish(buf, k):
        await_bytes(buf.at[pl.ds(0, n_chip - 1), core], sem_g_r.at[k])
        await_bytes(buf.at[pl.ds(0, n_chip - 1), core], sem_g_s.at[k])
        cp = pltpu.make_async_remote_copy(
            src_ref=buf.at[:, core],
            dst_ref=buf.at[:, core],
            send_sem=sem_d_s.at[k],
            recv_sem=sem_d_r.at[k],
            device_id=(p + 1 - 2 * core, y),
            device_id_type=MESH,
        )
        cp.start()
        return cp

    def unit(buf, temp, cat, keep):
        flat[...] = buf[...].reshape(flat.shape)
        for ct in range(n_ct):
            rows = pl.ds(ct * LANES, LANES)
            x = flat[pl.ds(ct, width, stride=n_ct), :]
            x = x * (1.0 / jnp.sqrt(jnp.sum(x * x, axis=0, keepdims=True) + EPS))
            if keep:
                hi, lo = split(x)
                zs_hi[:, rows] = hi
                zs_lo[:, rows] = lo
            xt = (x * (1.0 / temp)).T
            hi, lo = split(xt)
            cat[rows, 0:width] = hi
            cat[rows, width : 2 * width] = lo
            cat[rows, 2 * width : 3 * width] = hi

    def col_start(k):
        col_in[k, pl.ds(y, 1)] = col_out[k : k + 1]
        for i in range(1, n_y):
            pltpu.make_async_remote_copy(
                src_ref=col_out.at[k],
                dst_ref=col_in.at[k, y],
                send_sem=sem_c_s.at[k],
                recv_sem=sem_c_r.at[k],
                device_id=(p, lax.rem(y + i, n_y)),
                device_id_type=MESH,
            ).start()

    def col_finish(k):
        await_bytes(col_in.at[k, pl.ds(0, n_y - 1)], sem_c_r.at[k])
        total = col_in[k, 0]
        for i in range(1, n_y):
            total = total + col_in[k, i]
        ubuf[...] = 1.0 / total

    def row_start(k):
        row_in[k, pl.ds(p, 1)] = row_out[k : k + 1]

        def go(i, c):
            pltpu.make_async_remote_copy(
                src_ref=row_out.at[k],
                dst_ref=row_in.at[k, p],
                send_sem=sem_r_s.at[k],
                recv_sem=sem_r_r.at[k],
                device_id=(lax.rem(p + i, n_plane), y),
                device_id_type=MESH,
            ).start()
            return c

        lax.fori_loop(1, n_plane, go, 0)

    def row_finish(k):
        await_bytes(row_in.at[k, pl.ds(0, n_plane - 1)], sem_r_r.at[k])
        return jnp.sum(row_in[k], axis=0)

    def to_rows(k):
        for ct in range(n_ct):
            block = tcol[ct * LANES : (ct + 1) * LANES, :].T
            row_out[k, ct : ct + 1, :] = jnp.sum(block, axis=0, keepdims=True)

    def to_column(values):
        for ct in range(n_ct):
            row = jnp.broadcast_to(values[ct : ct + 1, :], (LANES, LANES))
            vcol[ct * LANES : (ct + 1) * LANES, :] = row.T

    chunk = 64

    def lane_fold(x):
        total = x[:, 0:LANES]
        for j in range(1, n_pt):
            total = total + x[:, j * LANES : (j + 1) * LANES]
        return total

    def scaled_fold(rows, mult):
        total = None
        for j in range(n_pt):
            x = e_ref[rows, j * LANES : (j + 1) * LANES]
            if mult is not None:
                x = x * mult[rows, j * LANES : (j + 1) * LANES]
            x = x * ubuf[j : j + 1, :]
            total = x if total is None else total + x
        return total

    def row_pass(k, mult):
        def go(i, c):
            rows = pl.ds(pl.multiple_of(i * chunk, chunk), chunk)
            tcol[rows, :] = scaled_fold(rows, mult)
            return c

        lax.fori_loop(0, crops // chunk, go, 0)
        to_rows(k)

    def col_pass(k):
        def go(i, acc):
            rows = pl.ds(pl.multiple_of(i * 32, 32), 32)
            v = vcol[rows, :]
            out = []
            for j in range(n_pt):
                x = e_ref[rows, j * LANES : (j + 1) * LANES] * v
                out.append(acc[j] + jnp.sum(x.reshape(4, 8, LANES), axis=0))
            return tuple(out)

        acc = lax.fori_loop(0, crops // 32, go, tuple(jnp.zeros((8, LANES), f32) for _ in range(n_pt)))
        for j in range(n_pt):
            col_out[k, j : j + 1, :] = jnp.sum(acc[j], axis=0, keepdims=True)

    gather_start(gt, 0)
    pair_t = gather_finish(gt, 0)
    gather_start(gs, 1)
    pair_t.wait()
    unit(gt, TEACHER_TEMP, zt_cat, False)

    def teacher_block(i, c):
        cols = pl.ds(pl.multiple_of(i * 256, 256), 256)
        e = jnp.exp(nn(zt_cat[...], w_cat[:, cols]))
        e_ref[:, cols] = e
        sums = jnp.sum(e, axis=0, keepdims=True)
        col_out[0, pl.ds(2 * i, 1), :] = sums[:, 0:LANES]
        col_out[0, pl.ds(2 * i + 1, 1), :] = sums[:, LANES : 2 * LANES]
        return c

    lax.fori_loop(0, protos // 256, teacher_block, 0)
    col_start(0)
    pair_s = gather_finish(gs, 1)
    col_finish(0)
    row_pass(0, None)
    row_start(0)

    pair_s.wait()
    unit(gs, STUDENT_TEMP, zs_cat, True)

    def student_block(i, c):
        cols = pl.ds(pl.multiple_of(i * 256, 256), 256)
        s = nn(zs_cat[...], w_cat[:, cols])
        s_log[:, cols] = s
        es_ref[:, cols] = jnp.exp(s)
        return c

    lax.fori_loop(0, protos // 256, student_block, 0)
    for k in (1, 2):
        to_column(1.0 / row_finish(k - 1))
        col_pass(k)
        col_start(k)
        if k == 1:
            def fold(i, c):
                rows = pl.ds(pl.multiple_of(i * chunk, chunk), chunk)
                tcol[rows, :] = lane_fold(es_ref[rows, :])
                return c

            lax.fori_loop(0, crops // chunk, fold, 0)
            to_rows(3)
            row_start(3)
        col_finish(k)
        row_pass(k, None)
        row_start(k)
    row_pass(4, s_log)
    row_start(4)
    last = row_finish(2)
    student_total = row_finish(3)
    cross = row_finish(4)
    to_column(scale / last)
    tv = scale / student_total
    for ct in range(n_ct):
        row = jnp.broadcast_to(tv[ct : ct + 1, :], (LANES, LANES))
        tcol[ct * LANES : (ct + 1) * LANES, :] = row.T
    loss_in[pl.ds(y, 1)] = (jnp.log(student_total) - cross / last)[None]
    for i in range(1, n_y):
        pltpu.make_async_remote_copy(
            src_ref=loss_in.at[y],
            dst_ref=loss_in.at[y],
            send_sem=sem_l_s.at[0],
            recv_sem=sem_l_r.at[0],
            device_id=(p, lax.rem(y + i, n_y)),
            device_id_type=MESH,
        ).start()

    def grad_block(i, c):
        rows = pl.ds(pl.multiple_of(i * 32, 32), 32)
        v = vcol[rows, :]
        t = tcol[rows, :]
        for j in range(n_pt):
            lanes = slice(j * LANES, (j + 1) * LANES)
            g = es_ref[rows, lanes] * t - e_ref[rows, lanes] * ubuf[j : j + 1, :] * v
            hi, lo = split(g)
            g_hi[rows, lanes] = hi
            g_lo[rows, lanes] = lo
        return c

    lax.fori_loop(0, crops // 32, grad_block, 0)

    gf_acc[...] = jnp.zeros_like(gf_acc)

    def feat_block(i, c):
        cols = pl.ds(pl.multiple_of(i * 512, 512), 512)
        w_hi = w_cat[0:width, cols]
        w_lo = w_cat[2 * width : 3 * width, cols]
        gf_acc[...] += nt(w_hi, g_hi[:, cols]) + nt(w_hi, g_lo[:, cols]) + nt(w_lo, g_hi[:, cols])
        return c

    lax.fori_loop(0, protos // 512, feat_block, 0)
    for ct in range(n_ct):
        rs_flat[pl.ds(ct, width, stride=n_ct), :] = gf_acc[:, ct * LANES : (ct + 1) * LANES]
    rs_src[...] = rs_flat[...].reshape(rs_src.shape)
    pair = pltpu.make_async_remote_copy(
        src_ref=rs_src.at[:, 1 - core],
        dst_ref=rs_pair,
        send_sem=sem_f_s.at[0],
        recv_sem=sem_f_r.at[0],
        device_id=(p + 1 - 2 * core, y),
        device_id_type=MESH,
    )
    pair.start()
    pair.wait()
    rs_pair[...] += rs_src[:, core]
    rs_in[pl.ds(chip, 1)] = rs_pair[pl.ds(chip, 1)]

    def scatter(i, c):
        other = lax.rem(chip + i, n_chip)
        pltpu.make_async_remote_copy(
            src_ref=rs_pair.at[other],
            dst_ref=rs_in.at[chip],
            send_sem=sem_f_s.at[1],
            recv_sem=sem_f_r.at[1],
            device_id=(other * 2 + core, y),
            device_id_type=MESH,
        ).start()
        return c

    lax.fori_loop(1, n_chip, scatter, 0)

    def proto_block(i, c):
        cols = pl.ds(pl.multiple_of(i * 256, 256), 256)
        a = g_hi[:, cols]
        gp_ref[:, cols] = nn(zs_hi[...], a) + nn(zs_lo[...], a) + nn(zs_hi[...], g_lo[:, cols])
        return c

    lax.fori_loop(0, protos // 256, proto_block, 0)

    await_bytes(loss_in.at[pl.ds(0, n_y - 1)], sem_l_r.at[0])
    loss_ref[0, 0] = jnp.sum(jnp.sum(loss_in[...], axis=0)) * (1.0 / crops_all)
    await_bytes(rs_in.at[pl.ds(0, n_chip - 1)], sem_f_r.at[1])
    total = jnp.sum(rs_in[...], axis=0)
    for j in range(feat):
        for ct in range(n_ct):
            k = n_ct * j + ct
            gf_ref[j : j + 1, ct * LANES : (ct + 1) * LANES] = total[k : k + 1, :]

    pair_t_sem = None
    await_bytes(loss_in.at[pl.ds(0, n_y - 1)], sem_l_s.at[0])
    await_bytes(rs_in.at[pl.ds(0, n_chip - 1)], sem_f_s.at[1])
    for k in range(3):
        await_bytes(col_in.at[k, pl.ds(0, n_y - 1)], sem_c_s.at[k])
    for k in range(5):
        await_bytes(row_in.at[k, pl.ds(0, n_plane - 1)], sem_r_s.at[k])


def on_device(n_y, n_chip, t, s, w):
    width, protos = w.shape
    feat, crops = t.shape
    n_ct = crops // LANES
    n_pt = protos // LANES
    n_plane = 2 * n_chip
    scale = math.sqrt(protos * n_plane) / STUDENT_TEMP
    vm = pltpu.VMEM
    dma = pltpu.SemaphoreType.DMA
    slots = (n_chip, 2, feat * n_ct, LANES)
    gf, gp, loss = pl.pallas_call(
        functools.partial(kernel, n_y, n_chip, scale, crops * n_y),
        out_shape=(
            jax.ShapeDtypeStruct((feat, crops), f32),
            jax.ShapeDtypeStruct((width, protos), f32),
            jax.ShapeDtypeStruct((1, 1), f32),
        ),
        in_specs=[pl.BlockSpec(memory_space=vm)] * 3,
        out_specs=(
            pl.BlockSpec(memory_space=vm),
            pl.BlockSpec(memory_space=vm),
            pl.BlockSpec(memory_space=pltpu.SMEM),
        ),
        scratch_shapes=[
            vm(slots, f32),
            vm(slots, f32),
            vm((width * n_ct, LANES), f32),
            vm((crops, 3 * width), bf16),
            vm((crops, 3 * width), bf16),
            vm((width, crops), bf16),
            vm((width, crops), bf16),
            vm((3 * width, protos), bf16),
            vm((crops, protos), f32),
            vm((crops, protos), f32),
            vm((crops, protos), f32),
            vm((crops, protos), bf16),
            vm((crops, protos), bf16),
            vm((crops, LANES), f32),
            vm((crops, LANES), f32),
            vm((3, n_pt, LANES), f32),
            vm((3, n_y, n_pt, LANES), f32),
            vm((n_pt, LANES), f32),
            vm((5, n_ct, LANES), f32),
            vm((5, n_plane, n_ct, LANES), f32),
            vm((width, crops), f32),
            vm((width * n_ct, LANES), f32),
            vm(slots, f32),
            vm((n_chip, feat * n_ct, LANES), f32),
            vm((n_chip, feat * n_ct, LANES), f32),
            vm((n_y, n_ct, LANES), f32),
            dma((2,)), dma((2,)), dma((2,)), dma((2,)), dma((3,)), dma((3,)), dma((5,)), dma((5,)),
            dma((2,)), dma((2,)), dma((1,)), dma((1,)),
        ],
        compiler_params=pltpu.CompilerParams(
            collective_id=0, has_side_effects=True, vmem_limit_bytes=60 * 2**20
        ),
    )(t, s, w)
    gp = lax.psum_scatter(gp, "crop", scatter_dimension=0, tiled=True)
    return gf, gp, loss.reshape(())


def solution(mesh):
    placed = (P("proto", "crop"), P("proto", "crop"), P(None, "proto"))
    n_y = mesh.shape["crop"]
    n_chip = mesh.shape["proto"] // 2
    return jax.shard_map(
        functools.partial(on_device, n_y, n_chip),
        mesh=mesh,
        in_specs=placed,
        out_specs=(P("proto", "crop"), P("crop", "proto"), P()),
        check_vma=False,
    )
```

time: 873 us -> 145 us (0.17)
  blocking collectives: 702 us -> 0 us
  Pallas kernels: 0 us -> 89.9 us
  waiting for transfers between devices: 89.9 us -> 38.8 us
  matrix products: 42.6 us -> 0 us
  other arithmetic: 15.8 us -> 0 us
    psum x8 -> x0, blocking collectives: 600 us -> none  [the longest x2 252 us: row_total(): return lax.psum(jnp.sum(values * scaling[None, :], axis=1), 'proto')]
    all_gather x2 -> x0, blocking collectives: 103 us -> none  [the longest x1 54.9 us: on_device(): lax.all_gather(teacher_feats, 'proto', axis=0, tiled=True)]
    psum x1 -> x0, waiting for transfers between devices: 89.9 us -> none  [on_device(): summed = lax.psum(whole, 'proto')]
    pallas_call x0 -> x1, Pallas kernels: none -> 89.9 us  [on_device(): pl.pallas_call(functools.partial(kernel, n_y, n_chip, scale, crops * n_y)...]
    dot_general x4 -> x0, matrix products: 42.6 us -> none  [the longest x2 21.9 us: project(): lax.dot_general(columns, weights, (((0,), (0,)), ((), ())), precision=hig...]
    reduce_scatter x1, waiting for transfers between devices: 0.01 us -> 38.8 us  [on_device(): gp = lax.psum_scatter(gp, 'crop', scatter_dimension=0, tiled=True)]
    reduce_sum x9 -> x0, other arithmetic: 15.7 us -> none  [the longest x2 5.11 us: row_total(): return lax.psum(jnp.sum(values * scaling[None, :], axis=1), 'proto')]
  transfers between devices with their start and end apart: 2 -> 1, of which waited for: 1 -> 1; matrix products, arithmetic and copies ran while one was open for 1% -> 0% of each run, Pallas kernels for 0% -> 0%
where the time goes in v1:
time: 145 us
  Pallas kernels  89.9 us (62%)
  waiting for transfers between devices  38.8 us (27%)
  between operations  15.7 us (11%)
    pallas_call x1, Pallas kernels, on_device(): pl.pallas_call(functools.partial(kernel, n_y, n_chip, scale, crops * n_y)...  89.9 us
    reduce_scatter x1, waiting for transfers between devices, on_device(): gp = lax.psum_scatter(gp, 'crop', scatter_dimension=0, tiled=True)  38.8 us
  transfers between devices with their start and end apart: 1, of which 1 were waited for; matrix products, arithmetic and copies ran while one was open for 0% of the time, Pallas kernels for 0%

profile of v1, /device:TPU:1, one launch (start us, length us, event | category | flops | bytes accessed | tf_op | source)
XLA Modules:
  0.0 145.0 jit_solution(18416887968709757521)
XLA Ops:
  7.2 0.0 reduce-scatter.2.cloned.1.call-start
  7.2 89.9 %shard_map.58 = (f32[6,512]{1,0:T(8,128)}, f32[384,2048]{1,0:T(8,128)}, f32[1,1]{1,0:T(1,128)}) custom-call(f32[6,512]{1,0:T(8,128)} %t_ref.1, f32[6,512]{1,0:T(8,128)} %s_ref.1, f32[384,2048]{1,0:T(8,128)} %w_ref.1), custom_call_target="tpu_custom_call" | custom-call | tf_op jit(solution)/shard_map/pallas_call | solution.py:383
  97.1 0.0 copy-start
  97.1 0.0 reduce-scatter.2.cloned.1.call-update
  97.1 38.8 %reduce-scatter.2.cloned.1.call-done = f32[96,2048]{1,0:T(8,128)} async-done(((f32[384,2048]{1,0:T(8,128)}), f32[96,2048]{1,0:T(8,128)}) %reduce-scatter.2.cloned.1.call-update) | async-done | bytes 786448 | tf_op jit(solution)/shard_map/reduce_scatter | solution.py:430
  135.9 0.0 copy-done
  135.9 0.6 copy.8
Async XLA Ops:
  7.2 128.7 %reduce-scatter.2.cloned.1.call-start = ((), (), s32[]{:S(2)}) async-start(), calls=%async_computation.1 | async-start | bytes 3932160 | tf_op jit(solution)/shard_map/reduce_scatter | solution.py:430
  97.1 38.8 %copy-start = (f32[6,512]{1,0:T(8,128)S(1)}, f32[6,512]{1,0:T(8,128)}, u32[]{:S(2)}) copy-start(f32[6,512]{1,0:T(8,128)} %get-tuple-element.12) | copy-start | bytes 36868
Sparse Core Ops, SparseCore 0:
  97.2 38.6 reduce-scatter.1

commit v2 on v1

--- a/solution.py
+++ b/solution.py
@@ -41,15 +41,17 @@
     gf_ref, gp_ref, loss_ref,
     gt, gs, flat, zt_cat, zs_cat, zs_hi, zs_lo, w_cat, e_ref, s_log, es_ref, g_hi, g_lo,
     tcol, vcol, col_out, col_in, ubuf, row_out, row_in, gf_acc, rs_flat, rs_src, rs_pair, rs_in,
-    loss_in,
+    loss_in, w_raw, part, relay, final,
     sem_g_s, sem_g_r, sem_d_s, sem_d_r, sem_c_s, sem_c_r, sem_r_s, sem_r_r, sem_f_s, sem_f_r,
-    sem_l_s, sem_l_r,
+    sem_l_s, sem_l_r, sem_w, sem_y_s, sem_y_r,
 ):
     p = lax.axis_index("proto")
     y = lax.axis_index("crop")
     chip = p // 2
     core = p % 2
-    width, protos = w_ref.shape
+    width, protos = w_raw.shape
+    w_copy = pltpu.make_async_copy(w_ref, w_raw, sem_w.at[0])
+    w_copy.start()
     crops = e_ref.shape[0]
     n_ct = crops // LANES
     n_pt = protos // LANES
@@ -74,7 +76,7 @@
 
     def prep_w(i, c):
         cols = pl.ds(pl.multiple_of(i * 256, 256), 256)
-        w = w_ref[:, cols]
+        w = w_raw[:, cols]
         w = w * (1.0 / jnp.sqrt(jnp.sum(w * w, axis=0, keepdims=True) + EPS))
         hi, lo = split(w)
         w_cat[0:width, cols] = hi
@@ -82,6 +84,7 @@
         w_cat[2 * width : 3 * width, cols] = lo
         return c
 
+    w_copy.wait()
     lax.fori_loop(0, protos // 256, prep_w, 0)
     pl.semaphore_wait(bar, n_plane - 1 + n_y - 1)
 
@@ -237,12 +240,11 @@
 
     lax.fori_loop(0, protos // 256, teacher_block, 0)
     col_start(0)
-    pair_s = gather_finish(gs, 1)
     col_finish(0)
     row_pass(0, None)
     row_start(0)
 
-    pair_s.wait()
+    gather_finish(gs, 1).wait()
     unit(gs, STUDENT_TEMP, zs_cat, True)
 
     def student_block(i, c):
@@ -273,36 +275,70 @@
     row_start(4)
     last = row_finish(2)
     student_total = row_finish(3)
-    cross = row_finish(4)
     to_column(scale / last)
     tv = scale / student_total
     for ct in range(n_ct):
         row = jnp.broadcast_to(tv[ct : ct + 1, :], (LANES, LANES))
         tcol[ct * LANES : (ct + 1) * LANES, :] = row.T
-    loss_in[pl.ds(y, 1)] = (jnp.log(student_total) - cross / last)[None]
-    for i in range(1, n_y):
+
+    ahead = lax.rem(y + 1, n_y)
+    across = lax.rem(y + 2, n_y)
+    behind = lax.rem(y + n_y - 1, n_y)
+    out_rows = width // n_y
+    half = 256
+    n_part = protos // (2 * half)
+
+    def rows_of(d):
+        return pl.ds(pl.multiple_of(d * out_rows, 8), out_rows)
+
+    def hop(src, dst, s, r, target):
         pltpu.make_async_remote_copy(
-            src_ref=loss_in.at[y],
-            dst_ref=loss_in.at[y],
-            send_sem=sem_l_s.at[0],
-            recv_sem=sem_l_r.at[0],
-            device_id=(p, lax.rem(y + i, n_y)),
-            device_id_type=MESH,
+            src_ref=src, dst_ref=dst, send_sem=s, recv_sem=r, device_id=(p, target), device_id_type=MESH
         ).start()
 
-    def grad_block(i, c):
-        rows = pl.ds(pl.multiple_of(i * 32, 32), 32)
-        v = vcol[rows, :]
-        t = tcol[rows, :]
-        for j in range(n_pt):
-            lanes = slice(j * LANES, (j + 1) * LANES)
-            g = es_ref[rows, lanes] * t - e_ref[rows, lanes] * ubuf[j : j + 1, :] * v
-            hi, lo = split(g)
-            g_hi[rows, lanes] = hi
-            g_lo[rows, lanes] = lo
-        return c
-
-    lax.fori_loop(0, crops // 32, grad_block, 0)
+    def proto_part(i):
+        base = i * 2 * half
+
+        def grad_block(r, c):
+            rows = pl.ds(pl.multiple_of(r * 64, 64), 64)
+            v = vcol[rows, :]
+            t = tcol[rows, :]
+            for j in range(2 * half // LANES):
+                lanes = slice(base + j * LANES, base + (j + 1) * LANES)
+                k = base // LANES + j
+                g = es_ref[rows, lanes] * t - e_ref[rows, lanes] * ubuf[k : k + 1, :] * v
+                hi, lo = split(g)
+                g_hi[rows, lanes] = hi
+                g_lo[rows, lanes] = lo
+            return c
+
+        lax.fori_loop(0, crops // 64, grad_block, 0)
+        for h in range(2):
+            lanes = slice(base + h * half, base + (h + 1) * half)
+            a = g_hi[:, lanes]
+            part[i, h] = nn(zs_hi[...], a) + nn(zs_lo[...], a) + nn(zs_hi[...], g_lo[:, lanes])
+        hop(part.at[i, 0, rows_of(across)], relay.at[i, 0], sem_y_s.at[i, 0], sem_y_r.at[i, 0], ahead)
+        hop(part.at[i, 1, rows_of(across)], relay.at[i, 1], sem_y_s.at[i, 1], sem_y_r.at[i, 1], behind)
+        hop(part.at[i, 1, rows_of(ahead)], final.at[i, 0, 1], sem_y_s.at[i, 2], sem_y_r.at[i, 2], ahead)
+        hop(part.at[i, 0, rows_of(behind)], final.at[i, 1, 0], sem_y_s.at[i, 3], sem_y_r.at[i, 3], behind)
+
+    def relay_part(i):
+        await_bytes(relay.at[i, 0], sem_y_r.at[i, 0])
+        relay[i, 0] += part[i, 0, rows_of(ahead)]
+        hop(relay.at[i, 0], final.at[i, 0, 0], sem_y_s.at[i, 4], sem_y_r.at[i, 2], ahead)
+        await_bytes(relay.at[i, 1], sem_y_r.at[i, 1])
+        relay[i, 1] += part[i, 1, rows_of(behind)]
+        hop(relay.at[i, 1], final.at[i, 1, 1], sem_y_s.at[i, 5], sem_y_r.at[i, 3], behind)
+
+    def final_part(i):
+        for side in range(2):
+            await_bytes(final.at[i, side], sem_y_r.at[i, 2 + side])
+        for h in range(2):
+            lanes = slice((2 * i + h) * half, (2 * i + h + 1) * half)
+            gp_ref[:, lanes] = part[i, h, rows_of(y)] + final[i, 0, h] + final[i, 1, h]
+
+    for i in range(n_part):
+        proto_part(i)
 
     gf_acc[...] = jnp.zeros_like(gf_acc)
 
@@ -326,6 +362,7 @@
         device_id_type=MESH,
     )
     pair.start()
+    relay_part(0)
     pair.wait()
     rs_pair[...] += rs_src[:, core]
     rs_in[pl.ds(chip, 1)] = rs_pair[pl.ds(chip, 1)]
@@ -343,25 +380,27 @@
         return c
 
     lax.fori_loop(1, n_chip, scatter, 0)
-
-    def proto_block(i, c):
-        cols = pl.ds(pl.multiple_of(i * 256, 256), 256)
-        a = g_hi[:, cols]
-        gp_ref[:, cols] = nn(zs_hi[...], a) + nn(zs_lo[...], a) + nn(zs_hi[...], g_lo[:, cols])
-        return c
-
-    lax.fori_loop(0, protos // 256, proto_block, 0)
-
-    await_bytes(loss_in.at[pl.ds(0, n_y - 1)], sem_l_r.at[0])
-    loss_ref[0, 0] = jnp.sum(jnp.sum(loss_in[...], axis=0)) * (1.0 / crops_all)
+    for i in range(1, n_part):
+        relay_part(i)
+    cross = row_finish(4)
+    loss_in[pl.ds(y, 1)] = (jnp.log(student_total) - cross / last)[None]
+    for i in range(1, n_y):
+        hop(loss_in.at[y], loss_in.at[y], sem_l_s.at[0], sem_l_r.at[0], lax.rem(y + i, n_y))
+
     await_bytes(rs_in.at[pl.ds(0, n_chip - 1)], sem_f_r.at[1])
     total = jnp.sum(rs_in[...], axis=0)
     for j in range(feat):
         for ct in range(n_ct):
             k = n_ct * j + ct
             gf_ref[j : j + 1, ct * LANES : (ct + 1) * LANES] = total[k : k + 1, :]
-
-    pair_t_sem = None
+    for i in range(n_part):
+        final_part(i)
+    await_bytes(loss_in.at[pl.ds(0, n_y - 1)], sem_l_r.at[0])
+    loss_ref[0, 0] = jnp.sum(jnp.sum(loss_in[...], axis=0)) * (1.0 / crops_all)
+
+    for i in range(n_part):
+        for k in range(6):
+            await_bytes(relay.at[i, 0], sem_y_s.at[i, k])
     await_bytes(loss_in.at[pl.ds(0, n_y - 1)], sem_l_s.at[0])
     await_bytes(rs_in.at[pl.ds(0, n_chip - 1)], sem_f_s.at[1])
     for k in range(3):
@@ -384,10 +423,14 @@
         functools.partial(kernel, n_y, n_chip, scale, crops * n_y),
         out_shape=(
             jax.ShapeDtypeStruct((feat, crops), f32),
-            jax.ShapeDtypeStruct((width, protos), f32),
+            jax.ShapeDtypeStruct((width // n_y, protos), f32),
             jax.ShapeDtypeStruct((1, 1), f32),
         ),
-        in_specs=[pl.BlockSpec(memory_space=vm)] * 3,
+        in_specs=[
+            pl.BlockSpec(memory_space=vm),
+            pl.BlockSpec(memory_space=vm),
+            pl.BlockSpec(memory_space=pl.ANY),
+        ],
         out_specs=(
             pl.BlockSpec(memory_space=vm),
             pl.BlockSpec(memory_space=vm),
@@ -420,14 +463,18 @@
             vm((n_chip, feat * n_ct, LANES), f32),
             vm((n_chip, feat * n_ct, LANES), f32),
             vm((n_y, n_ct, LANES), f32),
+            vm((width, protos), f32),
+            vm((protos // 512, 2, width, 256), f32),
+            vm((protos // 512, 2, width // n_y, 256), f32),
+            vm((protos // 512, 2, 2, width // n_y, 256), f32),
             dma((2,)), dma((2,)), dma((2,)), dma((2,)), dma((3,)), dma((3,)), dma((5,)), dma((5,)),
             dma((2,)), dma((2,)), dma((1,)), dma((1,)),
+            dma((1,)), dma((protos // 512, 6)), dma((protos // 512, 4)),
         ],
         compiler_params=pltpu.CompilerParams(
             collective_id=0, has_side_effects=True, vmem_limit_bytes=60 * 2**20
         ),
     )(t, s, w)
-    gp = lax.psum_scatter(gp, "crop", scatter_dimension=0, tiled=True)
     return gf, gp, loss.reshape(())
 
 

time: 145 us -> 103 us (0.71)
  waiting for transfers between devices: 38.8 us -> 0 us
  between operations: 15.7 us -> 2.4 us
  Pallas kernels: 89.9 us -> 97 us
  local copies, waits for them, and re-layouts: 0.61 us -> 3.39 us
    reduce_scatter x1 -> x0, waiting for transfers between devices: 38.8 us -> none  [on_device(): gp = lax.psum_scatter(gp, 'crop', scatter_dimension=0, tiled=True)]
    pallas_call x1, Pallas kernels: 89.9 us -> 97 us  [on_device(): pl.pallas_call(functools.partial(kernel, n_y, n_chip, scale, crops * n_y)...]
    unnamed x3 -> x2, local copies, waits for them, and re-layouts: 0.61 us -> 3.39 us
  transfers between devices with their start and end apart: 1 -> 0, of which waited for: 1 -> 0; matrix products, arithmetic and copies ran while one was open for 0% -> 0% of each run, Pallas kernels for 0% -> 0%
where the time goes in v2:
time: 103 us
  Pallas kernels  97 us (94%)
  local copies, waits for them, and re-layouts  3.39 us (3%)
  between operations  2.4 us (2%)
    pallas_call x1, Pallas kernels, on_device(): pl.pallas_call(functools.partial(kernel, n_y, n_chip, scale, crops * n_y)...  97 us
    unnamed x2, local copies, waits for them, and re-layouts  3.39 us

profile of v2, /device:TPU:1, one launch (start us, length us, event | category | flops | bytes accessed | tf_op | source)
XLA Modules:
  0.0 102.8 jit_solution(4720094158609669882)
XLA Ops:
  0.6 97.0 %shard_map.58 = (f32[6,512]{1,0:T(8,128)}, f32[96,2048]{1,0:T(8,128)}, f32[1,1]{1,0:T(1,128)}) custom-call(f32[6,512]{1,0:T(8,128)} %t_ref.1, f32[6,512]{1,0:T(8,128)} %s_ref.1, f32[384,2048]{1,0:T(8,128)} %w_ref.1), custom_call_target="tpu_custom_call" | custom-call | tf_op jit(solution)/shard_map/pallas_call | solution.py:422
  97.7 1.3 %copy.9 = f32[6,512]{1,0:T(8,128)} copy(f32[6,512]{1,0:T(8,128)} %get-tuple-element.12) | data formatting | bytes 24576
  99.0 2.1 %copy.10 = f32[96,2048]{1,0:T(8,128)} copy(f32[96,2048]{1,0:T(8,128)} %get-tuple-element.13) | data formatting | bytes 1572864

commit v3 on v1

--- a/solution.py
+++ b/solution.py
@@ -40,21 +40,34 @@
     t_ref, s_ref, w_ref,
     gf_ref, gp_ref, loss_ref,
     gt, gs, flat, zt_cat, zs_cat, zs_hi, zs_lo, w_cat, e_ref, s_log, es_ref, g_hi, g_lo,
+    er, esr, gr_hi, gr_lo, far, vfar, tfar,
     tcol, vcol, col_out, col_in, ubuf, row_out, row_in, gf_acc, rs_flat, rs_src, rs_pair, rs_in,
-    loss_in,
+    loss_in, w_raw, part, final,
     sem_g_s, sem_g_r, sem_d_s, sem_d_r, sem_c_s, sem_c_r, sem_r_s, sem_r_r, sem_f_s, sem_f_r,
-    sem_l_s, sem_l_r,
+    sem_l_s, sem_l_r, sem_w, sem_y_s, sem_y_r, sem_a_s, sem_a_r,
+    sem_e_s, sem_e_r, sem_v_s, sem_v_r,
 ):
     p = lax.axis_index("proto")
     y = lax.axis_index("crop")
     chip = p // 2
     core = p % 2
-    width, protos = w_ref.shape
+    width, protos = w_raw.shape
+    w_copy = pltpu.make_async_copy(w_ref, w_raw, sem_w.at[0])
+    w_copy.start()
     crops = e_ref.shape[0]
     n_ct = crops // LANES
     n_pt = protos // LANES
     feat = width // (2 * n_chip)
     n_plane = 2 * n_chip
+    n_z = 8
+    n_x = n_chip // n_z
+    chip_x = chip // n_z
+    chip_z = chip % n_z
+    groups = (0, 1, 3, 2)
+    ahead = lax.rem(y + 1, n_y)
+    across = lax.rem(y + 2, n_y)
+    behind = lax.rem(y + n_y - 1, n_y)
+    mine = protos // n_y
 
     bar = pltpu.get_barrier_semaphore()
 
@@ -70,11 +83,11 @@
         for j in range(feat):
             for ct in range(n_ct):
                 k = n_ct * j + ct
-                dst[chip, core, k : k + 1, :] = src[j : j + 1, ct * LANES : (ct + 1) * LANES]
+                dst[0, chip, core, k : k + 1, :] = src[j : j + 1, ct * LANES : (ct + 1) * LANES]
 
     def prep_w(i, c):
         cols = pl.ds(pl.multiple_of(i * 256, 256), 256)
-        w = w_ref[:, cols]
+        w = w_raw[:, cols]
         w = w * (1.0 / jnp.sqrt(jnp.sum(w * w, axis=0, keepdims=True) + EPS))
         hi, lo = split(w)
         w_cat[0:width, cols] = hi
@@ -82,53 +95,88 @@
         w_cat[2 * width : 3 * width, cols] = lo
         return c
 
+    w_copy.wait()
     lax.fori_loop(0, protos // 256, prep_w, 0)
     pl.semaphore_wait(bar, n_plane - 1 + n_y - 1)
 
+    def remote(src, dst, s, r, plane, crop):
+        copy = pltpu.make_async_remote_copy(
+            src_ref=src, dst_ref=dst, send_sem=s, recv_sem=r, device_id=(plane, crop), device_id_type=MESH
+        )
+        copy.start()
+        return copy
+
+    sibling = p + 1 - 2 * core
+
     def gather_start(buf, k):
-        def go(i, c):
-            other = lax.rem(chip + i, n_chip)
-            pltpu.make_async_remote_copy(
-                src_ref=buf.at[chip, core],
-                dst_ref=buf.at[chip, core],
-                send_sem=sem_g_s.at[k],
-                recv_sem=sem_g_r.at[k],
-                device_id=(other * 2 + core, y),
-                device_id_type=MESH,
-            ).start()
-            return c
-
-        lax.fori_loop(1, n_chip, go, 0)
+        for dx in groups:
+            def go(dz, c):
+                other = lax.rem(chip_x + dx, n_x) * n_z + lax.rem(chip_z + dz, n_z)
+                here = buf.at[0, chip, core]
+                remote(here, here, sem_g_s.at[k], sem_g_r.at[k, dx], other * 2 + core, y)
+                return c
+
+            lax.fori_loop(1 if dx == 0 else 0, n_z, go, 0)
+
+    def slots_of(dx):
+        return pl.ds(pl.multiple_of(lax.rem(chip_x + n_x - dx, n_x) * n_z, n_z), n_z)
+
+    def gather_group(buf, k, dx):
+        got = buf.at[0, pl.ds(0, n_z - 1 if dx == 0 else n_z), core]
+        await_bytes(got, sem_g_r.at[k, dx])
+        block = buf.at[0, slots_of(dx), core]
+        remote(block, block, sem_d_s.at[k], sem_d_r.at[k], sibling, y)
+
+    def spread_group(buf, k, dx):
+        block = buf.at[0, slots_of(dx), core]
+        remote(block, buf.at[n_y - 1, slots_of(dx), core], sem_a_s.at[k, 0], sem_a_r.at[k, 0], p, ahead)
+        remote(block, buf.at[1, slots_of(dx), core], sem_a_s.at[k, 1], sem_a_r.at[k, 1], p, behind)
 
     def gather_finish(buf, k):
-        await_bytes(buf.at[pl.ds(0, n_chip - 1), core], sem_g_r.at[k])
-        await_bytes(buf.at[pl.ds(0, n_chip - 1), core], sem_g_s.at[k])
-        cp = pltpu.make_async_remote_copy(
-            src_ref=buf.at[:, core],
-            dst_ref=buf.at[:, core],
-            send_sem=sem_d_s.at[k],
-            recv_sem=sem_d_r.at[k],
-            device_id=(p + 1 - 2 * core, y),
-            device_id_type=MESH,
-        )
-        cp.start()
-        return cp
-
-    def unit(buf, temp, cat, keep):
-        flat[...] = buf[...].reshape(flat.shape)
+        await_bytes(buf.at[0, :, core], sem_d_r.at[k])
+
+    def share(buf, k, rel):
+        block = buf.at[rel, :, core]
+        remote(block, block, sem_e_s.at[k, rel - 1], sem_e_r.at[k, rel - 1], sibling, y)
+
+    def near_finish(buf, k):
+        await_bytes(buf.at[n_y - 1, :, core], sem_a_r.at[k, 0])
+        await_bytes(buf.at[1, :, core], sem_a_r.at[k, 1])
+        share(buf, k, 1)
+        share(buf, k, 3)
+
+    def relay(buf, k):
+        low, high = pl.ds(0, n_chip // 2), pl.ds(n_chip // 2, n_chip // 2)
+        remote(buf.at[3, low, core], buf.at[2, low, core], sem_a_s.at[k, 2], sem_a_r.at[k, 2], p, ahead)
+        remote(buf.at[1, high, core], buf.at[2, high, core], sem_a_s.at[k, 3], sem_a_r.at[k, 3], p, behind)
+
+    def far_finish(buf, k):
+        for i in (2, 3):
+            await_bytes(buf.at[2, pl.ds(0, n_chip // 2), core], sem_a_r.at[k, i])
+        share(buf, k, 2)
+
+    def unit(buf, rel, temp, cat, keep):
+        flat[...] = buf[rel].reshape(flat.shape)
         for ct in range(n_ct):
             rows = pl.ds(ct * LANES, LANES)
             x = flat[pl.ds(ct, width, stride=n_ct), :]
             x = x * (1.0 / jnp.sqrt(jnp.sum(x * x, axis=0, keepdims=True) + EPS))
             if keep:
                 hi, lo = split(x)
-                zs_hi[:, rows] = hi
-                zs_lo[:, rows] = lo
+                zs_hi[rel, :, rows] = hi
+                zs_lo[rel, :, rows] = lo
             xt = (x * (1.0 / temp)).T
             hi, lo = split(xt)
             cat[rows, 0:width] = hi
             cat[rows, width : 2 * width] = lo
             cat[rows, 2 * width : 3 * width] = hi
+
+    def other_block(buf, k, rel, temp, dst, keep):
+        await_bytes(buf.at[rel, :, core], sem_e_r.at[k, rel - 1])
+        unit(buf, rel, temp, zt_cat, keep)
+        for h in range(mine // 256):
+            cols = pl.ds(pl.multiple_of(y * mine + h * 256, 256), 256)
+            dst[rel - 1, :, h * 256 : (h + 1) * 256] = jnp.exp(nn(zt_cat[...], w_cat[:, cols]))
 
     def col_start(k):
         col_in[k, pl.ds(y, 1)] = col_out[k : k + 1]
@@ -221,10 +269,12 @@
             col_out[k, j : j + 1, :] = jnp.sum(acc[j], axis=0, keepdims=True)
 
     gather_start(gt, 0)
-    pair_t = gather_finish(gt, 0)
+    for dx in groups:
+        gather_group(gt, 0, dx)
+        spread_group(gt, 0, dx)
     gather_start(gs, 1)
-    pair_t.wait()
-    unit(gt, TEACHER_TEMP, zt_cat, False)
+    gather_finish(gt, 0)
+    unit(gt, 0, TEACHER_TEMP, zt_cat, False)
 
     def teacher_block(i, c):
         cols = pl.ds(pl.multiple_of(i * 256, 256), 256)
@@ -237,13 +287,17 @@
 
     lax.fori_loop(0, protos // 256, teacher_block, 0)
     col_start(0)
-    pair_s = gather_finish(gs, 1)
+    near_finish(gt, 0)
     col_finish(0)
     row_pass(0, None)
     row_start(0)
-
-    pair_s.wait()
-    unit(gs, STUDENT_TEMP, zs_cat, True)
+    relay(gt, 0)
+
+    for dx in groups:
+        gather_group(gs, 1, dx)
+    spread_group(gs, 1, 0)
+    gather_finish(gs, 1)
+    unit(gs, 0, STUDENT_TEMP, zs_cat, True)
 
     def student_block(i, c):
         cols = pl.ds(pl.multiple_of(i * 256, 256), 256)
@@ -266,32 +320,42 @@
             lax.fori_loop(0, crops // chunk, fold, 0)
             to_rows(3)
             row_start(3)
+            other_block(gt, 0, 1, TEACHER_TEMP, er, False)
+            far_finish(gt, 0)
+        else:
+            near_finish(gs, 1)
         col_finish(k)
         row_pass(k, None)
         row_start(k)
+        if k == 1:
+            for dx in groups[1:]:
+                spread_group(gs, 1, dx)
+            other_block(gt, 0, 3, TEACHER_TEMP, er, False)
+            other_block(gt, 0, 2, TEACHER_TEMP, er, False)
+        else:
+            relay(gs, 1)
     row_pass(4, s_log)
     row_start(4)
+    other_block(gs, 1, 1, STUDENT_TEMP, esr, True)
+    other_block(gs, 1, 3, STUDENT_TEMP, esr, True)
     last = row_finish(2)
     student_total = row_finish(3)
-    cross = row_finish(4)
-    to_column(scale / last)
-    tv = scale / student_total
-    for ct in range(n_ct):
-        row = jnp.broadcast_to(tv[ct : ct + 1, :], (LANES, LANES))
-        tcol[ct * LANES : (ct + 1) * LANES, :] = row.T
-    loss_in[pl.ds(y, 1)] = (jnp.log(student_total) - cross / last)[None]
+    far[0, 0:n_ct, :] = scale / last
+    far[0, n_ct : 2 * n_ct, :] = scale / student_total
     for i in range(1, n_y):
-        pltpu.make_async_remote_copy(
-            src_ref=loss_in.at[y],
-            dst_ref=loss_in.at[y],
-            send_sem=sem_l_s.at[0],
-            recv_sem=sem_l_r.at[0],
-            device_id=(p, lax.rem(y + i, n_y)),
-            device_id_type=MESH,
-        ).start()
-
-    def grad_block(i, c):
-        rows = pl.ds(pl.multiple_of(i * 32, 32), 32)
+        remote(far.at[0], far.at[n_y - i], sem_v_s.at[0], sem_v_r.at[0], p, lax.rem(y + i, n_y))
+
+    def spread_columns(rel, v_dst, t_dst):
+        for ct in range(n_ct):
+            rows = slice(ct * LANES, (ct + 1) * LANES)
+            for dst, k in ((v_dst, ct), (t_dst, n_ct + ct)):
+                row = jnp.broadcast_to(far[rel, k : k + 1, :], (LANES, LANES))
+                dst[rows, :] = row.T
+
+    spread_columns(0, vcol, tcol)
+
+    def grad_block(r, c):
+        rows = pl.ds(pl.multiple_of(r * 32, 32), 32)
         v = vcol[rows, :]
         t = tcol[rows, :]
         for j in range(n_pt):
@@ -326,6 +390,11 @@
         device_id_type=MESH,
     )
     pair.start()
+    cross = row_finish(4)
+    loss_in[pl.ds(y, 1)] = (jnp.log(student_total) - cross / last)[None]
+    for i in range(1, n_y):
+        remote(loss_in.at[y], loss_in.at[y], sem_l_s.at[0], sem_l_r.at[0], p, lax.rem(y + i, n_y))
+    far_finish(gs, 1)
     pair.wait()
     rs_pair[...] += rs_src[:, core]
     rs_in[pl.ds(chip, 1)] = rs_pair[pl.ds(chip, 1)]
@@ -343,25 +412,77 @@
         return c
 
     lax.fori_loop(1, n_chip, scatter, 0)
-
-    def proto_block(i, c):
-        cols = pl.ds(pl.multiple_of(i * 256, 256), 256)
-        a = g_hi[:, cols]
-        gp_ref[:, cols] = nn(zs_hi[...], a) + nn(zs_lo[...], a) + nn(zs_hi[...], g_lo[:, cols])
-        return c
-
-    lax.fori_loop(0, protos // 256, proto_block, 0)
-
-    await_bytes(loss_in.at[pl.ds(0, n_y - 1)], sem_l_r.at[0])
-    loss_ref[0, 0] = jnp.sum(jnp.sum(loss_in[...], axis=0)) * (1.0 / crops_all)
+    other_block(gs, 1, 2, STUDENT_TEMP, esr, True)
+    await_bytes(far.at[pl.ds(1, n_y - 1)], sem_v_r.at[0])
+    for rel in range(1, n_y):
+        spread_columns(rel, vfar.at[rel - 1], tfar.at[rel - 1])
+
+    out_rows = width // n_y
+    half = 256
+
+    def rows_of(d):
+        return pl.ds(pl.multiple_of(d * out_rows, 8), out_rows)
+
+    def proto_part(h):
+        base = pl.multiple_of(y * mine + h * half, half)
+        lanes_r = slice(h * half, (h + 1) * half)
+        own = pl.ds(base, half)
+        for rel in range(1, n_y):
+            def go(r, c):
+                rows = pl.ds(pl.multiple_of(r * 64, 64), 64)
+                v = vfar[rel - 1, rows, :]
+                t = tfar[rel - 1, rows, :]
+                for j in range(half // LANES):
+                    lanes = slice(h * half + j * LANES, h * half + (j + 1) * LANES)
+                    u = ubuf[pl.ds(y * (mine // LANES) + h * (half // LANES) + j, 1), :]
+                    g = esr[rel - 1, rows, lanes] * t - er[rel - 1, rows, lanes] * u * v
+                    hi, lo = split(g)
+                    gr_hi[rel - 1, rows, lanes] = hi
+                    gr_lo[rel - 1, rows, lanes] = lo
+                return c
+
+            lax.fori_loop(0, crops // 64, go, 0)
+        total = None
+        for rel in range(n_y):
+            if rel == 0:
+                a, b = g_hi[:, own], g_lo[:, own]
+            else:
+                a, b = gr_hi[rel - 1, :, lanes_r], gr_lo[rel - 1, :, lanes_r]
+            piece = nn(zs_hi[rel], a) + nn(zs_lo[rel], a) + nn(zs_hi[rel], b)
+            total = piece if total is None else total + piece
+        part[h] = total
+        final[h, pl.ds(y, 1)] = part[h, rows_of(y)][None]
+        for i in range(1, n_y):
+            to = lax.rem(y + i, n_y)
+            remote(part.at[h, rows_of(to)], final.at[h, y], sem_y_s.at[h], sem_y_r.at[h], p, to)
+
+    for h in range(mine // half):
+        proto_part(h)
+
     await_bytes(rs_in.at[pl.ds(0, n_chip - 1)], sem_f_r.at[1])
     total = jnp.sum(rs_in[...], axis=0)
     for j in range(feat):
         for ct in range(n_ct):
             k = n_ct * j + ct
             gf_ref[j : j + 1, ct * LANES : (ct + 1) * LANES] = total[k : k + 1, :]
-
-    pair_t_sem = None
+    for h in range(mine // half):
+        await_bytes(final.at[h, pl.ds(0, n_y - 1)], sem_y_r.at[h])
+        for q in range(n_y):
+            gp_ref[:, q * mine + h * half : q * mine + (h + 1) * half] = final[h, q]
+    await_bytes(loss_in.at[pl.ds(0, n_y - 1)], sem_l_r.at[0])
+    loss_ref[0, 0] = jnp.sum(jnp.sum(loss_in[...], axis=0)) * (1.0 / crops_all)
+
+    for k, buf in ((0, gt), (1, gs)):
+        await_bytes(buf.at[0, pl.ds(0, n_chip - 1), core], sem_g_s.at[k])
+        await_bytes(buf.at[0, :, core], sem_d_s.at[k])
+        for i in range(2):
+            await_bytes(buf.at[0, :, core], sem_a_s.at[k, i])
+            await_bytes(buf.at[0, pl.ds(0, n_chip // 2), core], sem_a_s.at[k, 2 + i])
+        for i in range(n_y - 1):
+            await_bytes(buf.at[0, :, core], sem_e_s.at[k, i])
+    await_bytes(far.at[pl.ds(1, n_y - 1)], sem_v_s.at[0])
+    for h in range(mine // half):
+        await_bytes(final.at[h, pl.ds(0, n_y - 1)], sem_y_s.at[h])
     await_bytes(loss_in.at[pl.ds(0, n_y - 1)], sem_l_s.at[0])
     await_bytes(rs_in.at[pl.ds(0, n_chip - 1)], sem_f_s.at[1])
     for k in range(3):
@@ -380,33 +501,45 @@
     vm = pltpu.VMEM
     dma = pltpu.SemaphoreType.DMA
     slots = (n_chip, 2, feat * n_ct, LANES)
+    mine = protos // n_y
     gf, gp, loss = pl.pallas_call(
         functools.partial(kernel, n_y, n_chip, scale, crops * n_y),
         out_shape=(
             jax.ShapeDtypeStruct((feat, crops), f32),
-            jax.ShapeDtypeStruct((width, protos), f32),
+            jax.ShapeDtypeStruct((width // n_y, protos), f32),
             jax.ShapeDtypeStruct((1, 1), f32),
         ),
-        in_specs=[pl.BlockSpec(memory_space=vm)] * 3,
+        in_specs=[
+            pl.BlockSpec(memory_space=vm),
+            pl.BlockSpec(memory_space=vm),
+            pl.BlockSpec(memory_space=pl.ANY),
+        ],
         out_specs=(
             pl.BlockSpec(memory_space=vm),
             pl.BlockSpec(memory_space=vm),
             pl.BlockSpec(memory_space=pltpu.SMEM),
         ),
         scratch_shapes=[
-            vm(slots, f32),
-            vm(slots, f32),
+            vm((n_y,) + slots, f32),
+            vm((n_y,) + slots, f32),
             vm((width * n_ct, LANES), f32),
             vm((crops, 3 * width), bf16),
             vm((crops, 3 * width), bf16),
-            vm((width, crops), bf16),
-            vm((width, crops), bf16),
+            vm((n_y, width, crops), bf16),
+            vm((n_y, width, crops), bf16),
             vm((3 * width, protos), bf16),
             vm((crops, protos), f32),
             vm((crops, protos), f32),
             vm((crops, protos), f32),
             vm((crops, protos), bf16),
             vm((crops, protos), bf16),
+            vm((n_y - 1, crops, mine), f32),
+            vm((n_y - 1, crops, mine), f32),
+            vm((n_y - 1, crops, mine), bf16),
+            vm((n_y - 1, crops, mine), bf16),
+            vm((n_y, 2 * n_ct, LANES), f32),
+            vm((n_y - 1, crops, LANES), f32),
+            vm((n_y - 1, crops, LANES), f32),
             vm((crops, LANES), f32),
             vm((crops, LANES), f32),
             vm((3, n_pt, LANES), f32),
@@ -420,14 +553,18 @@
             vm((n_chip, feat * n_ct, LANES), f32),
             vm((n_chip, feat * n_ct, LANES), f32),
             vm((n_y, n_ct, LANES), f32),
-            dma((2,)), dma((2,)), dma((2,)), dma((2,)), dma((3,)), dma((3,)), dma((5,)), dma((5,)),
+            vm((width, protos), f32),
+            vm((mine // 256, width, 256), f32),
+            vm((mine // 256, n_y, width // n_y, 256), f32),
+            dma((2,)), dma((2, 4)), dma((2,)), dma((2,)), dma((3,)), dma((3,)), dma((5,)), dma((5,)),
             dma((2,)), dma((2,)), dma((1,)), dma((1,)),
+            dma((1,)), dma((mine // 256,)), dma((mine // 256,)), dma((2, 4)), dma((2, 4)),
+            dma((2, 3)), dma((2, 3)), dma((1,)), dma((1,)),
         ],
         compiler_params=pltpu.CompilerParams(
             collective_id=0, has_side_effects=True, vmem_limit_bytes=60 * 2**20
         ),
     )(t, s, w)
-    gp = lax.psum_scatter(gp, "crop", scatter_dimension=0, tiled=True)
     return gf, gp, loss.reshape(())
 
 

time: 145 us -> 97.2 us (0.67)
  waiting for transfers between devices: 38.8 us -> 0 us
  between operations: 15.7 us -> 2.4 us
  local copies, waits for them, and re-layouts: 0.61 us -> 3.39 us
    reduce_scatter x1 -> x0, waiting for transfers between devices: 38.8 us -> none  [on_device(): gp = lax.psum_scatter(gp, 'crop', scatter_dimension=0, tiled=True)]
    unnamed x3 -> x2, local copies, waits for them, and re-layouts: 0.61 us -> 3.39 us
  transfers between devices with their start and end apart: 1 -> 0, of which waited for: 1 -> 0; matrix products, arithmetic and copies ran while one was open for 0% -> 0% of each run, Pallas kernels for 0% -> 0%
where the time goes in v3:
time: 97.2 us; the launch traced here: 96.8 us
  Pallas kernels  91 us (94%)
  local copies, waits for them, and re-layouts  3.39 us (3%)
  between operations  2.4 us (2%)
    pallas_call x1, Pallas kernels, on_device(): pl.pallas_call(functools.partial(kernel, n_y, n_chip, scale, crops * n_y)...  91 us
    unnamed x2, local copies, waits for them, and re-layouts  3.39 us

profile of v3, /device:TPU:1, one launch (start us, length us, event | category | flops | bytes accessed | tf_op | source)
XLA Modules:
  0.0 96.8 jit_solution(8091355839787623830)
XLA Ops:
  0.6 91.0 %shard_map.58 = (f32[6,512]{1,0:T(8,128)}, f32[96,2048]{1,0:T(8,128)}, f32[1,1]{1,0:T(1,128)}) custom-call(f32[6,512]{1,0:T(8,128)} %t_ref.1, f32[6,512]{1,0:T(8,128)} %s_ref.1, f32[384,2048]{1,0:T(8,128)} %w_ref.1), custom_call_target="tpu_custom_call" | custom-call | tf_op jit(solution)/shard_map/pallas_call | solution.py:505
  91.6 1.3 %copy.9 = f32[6,512]{1,0:T(8,128)} copy(f32[6,512]{1,0:T(8,128)} %get-tuple-element.12) | data formatting | bytes 24576
  92.9 2.1 %copy.10 = f32[96,2048]{1,0:T(8,128)} copy(f32[96,2048]{1,0:T(8,128)} %get-tuple-element.13) | data formatting | bytes 1572864

commit v4 on v3

--- a/solution.py
+++ b/solution.py
@@ -39,19 +39,20 @@
     n_y, n_chip, scale, crops_all,
     t_ref, s_ref, w_ref,
     gf_ref, gp_ref, loss_ref,
-    gt, gs, flat, zt_cat, zs_cat, zs_hi, zs_lo, w_cat, e_ref, s_log, es_ref, g_hi, g_lo,
-    er, esr, gr_hi, gr_lo, far, vfar, tfar,
-    tcol, vcol, col_out, col_in, ubuf, row_out, row_in, gf_acc, rs_flat, rs_src, rs_pair, rs_in,
-    loss_in, w_raw, part, final,
+    gt, gs, flat, zt_cat, zs_cat, z_cat, w_cat, e_ref, s_log, es_ref, g_hi, g_lo,
+    er, esr, g_cat, far, vfar, tfar, a1, a2,
+    tcol, vcol, col_out, col_in, ubuf, row_out, row_in, rs_flat, rs_src, rs_pair, rs_in,
+    loss_in, part, final,
     sem_g_s, sem_g_r, sem_d_s, sem_d_r, sem_c_s, sem_c_r, sem_r_s, sem_r_r, sem_f_s, sem_f_r,
     sem_l_s, sem_l_r, sem_w, sem_y_s, sem_y_r, sem_a_s, sem_a_r,
-    sem_e_s, sem_e_r, sem_v_s, sem_v_r,
+    sem_e_s, sem_e_r, sem_v_s, sem_v_r, sem_x_s,
 ):
     p = lax.axis_index("proto")
     y = lax.axis_index("crop")
     chip = p // 2
     core = p % 2
-    width, protos = w_raw.shape
+    width, protos = w_ref.shape
+    w_raw = s_log.at[0:width]
     w_copy = pltpu.make_async_copy(w_ref, w_raw, sem_w.at[0])
     w_copy.start()
     crops = e_ref.shape[0]
@@ -63,19 +64,27 @@
     n_x = n_chip // n_z
     chip_x = chip // n_z
     chip_z = chip % n_z
-    groups = (0, 1, 3, 2)
+    groups = (0, 2, 1, 3)
     ahead = lax.rem(y + 1, n_y)
     across = lax.rem(y + 2, n_y)
     behind = lax.rem(y + n_y - 1, n_y)
     mine = protos // n_y
+    sibling = p + 1 - 2 * core
 
     bar = pltpu.get_barrier_semaphore()
 
-    def greet_plane(i, c):
-        pl.semaphore_signal(bar, inc=1, device_id=(lax.rem(p + i, n_plane), y), device_id_type=MESH)
-        return c
-
-    lax.fori_loop(1, n_plane, greet_plane, 0)
+    def plane_peers(go):
+        def step(i, c):
+            go(lax.rem(p + i, n_plane))
+            return c
+
+        lax.fori_loop(24, n_plane, step, 0)
+        lax.fori_loop(1, 24, step, 0)
+
+    def greet(other):
+        pl.semaphore_signal(bar, inc=1, device_id=(other, y), device_id_type=MESH)
+
+    plane_peers(greet)
     for i in range(1, n_y):
         pl.semaphore_signal(bar, inc=1, device_id=(p, lax.rem(y + i, n_y)), device_id_type=MESH)
 
@@ -95,8 +104,6 @@
         w_cat[2 * width : 3 * width, cols] = lo
         return c
 
-    w_copy.wait()
-    lax.fori_loop(0, protos // 256, prep_w, 0)
     pl.semaphore_wait(bar, n_plane - 1 + n_y - 1)
 
     def remote(src, dst, s, r, plane, crop):
@@ -106,10 +113,8 @@
         copy.start()
         return copy
 
-    sibling = p + 1 - 2 * core
-
     def gather_start(buf, k):
-        for dx in groups:
+        for dx in groups[:2]:
             def go(dz, c):
                 other = lax.rem(chip_x + dx, n_x) * n_z + lax.rem(chip_z + dz, n_z)
                 here = buf.at[0, chip, core]
@@ -125,6 +130,10 @@
         got = buf.at[0, pl.ds(0, n_z - 1 if dx == 0 else n_z), core]
         await_bytes(got, sem_g_r.at[k, dx])
         block = buf.at[0, slots_of(dx), core]
+        if dx == 0:
+            for far_x in (1, 3):
+                over = lax.rem(chip_x + far_x, n_x) * n_z + chip_z
+                remote(block, block, sem_x_s.at[k], sem_g_r.at[k, far_x], over * 2 + core, y)
         remote(block, block, sem_d_s.at[k], sem_d_r.at[k], sibling, y)
 
     def spread_group(buf, k, dx):
@@ -163,8 +172,10 @@
             x = x * (1.0 / jnp.sqrt(jnp.sum(x * x, axis=0, keepdims=True) + EPS))
             if keep:
                 hi, lo = split(x)
-                zs_hi[rel, :, rows] = hi
-                zs_lo[rel, :, rows] = lo
+                base = rel * 3 * crops + ct * LANES
+                z_cat[:, base : base + LANES] = hi
+                z_cat[:, crops + base : crops + base + LANES] = lo
+                z_cat[:, 2 * crops + base : 2 * crops + base + LANES] = hi
             xt = (x * (1.0 / temp)).T
             hi, lo = split(xt)
             cat[rows, 0:width] = hi
@@ -174,9 +185,8 @@
     def other_block(buf, k, rel, temp, dst, keep):
         await_bytes(buf.at[rel, :, core], sem_e_r.at[k, rel - 1])
         unit(buf, rel, temp, zt_cat, keep)
-        for h in range(mine // 256):
-            cols = pl.ds(pl.multiple_of(y * mine + h * 256, 256), 256)
-            dst[rel - 1, :, h * 256 : (h + 1) * 256] = jnp.exp(nn(zt_cat[...], w_cat[:, cols]))
+        cols = pl.ds(pl.multiple_of(y * mine, mine), mine)
+        dst[rel - 1] = jnp.exp(nn(zt_cat[...], w_cat[:, cols]))
 
     def col_start(k):
         col_in[k, pl.ds(y, 1)] = col_out[k : k + 1]
@@ -200,18 +210,10 @@
     def row_start(k):
         row_in[k, pl.ds(p, 1)] = row_out[k : k + 1]
 
-        def go(i, c):
-            pltpu.make_async_remote_copy(
-                src_ref=row_out.at[k],
-                dst_ref=row_in.at[k, p],
-                send_sem=sem_r_s.at[k],
-                recv_sem=sem_r_r.at[k],
-                device_id=(lax.rem(p + i, n_plane), y),
-                device_id_type=MESH,
-            ).start()
-            return c
-
-        lax.fori_loop(1, n_plane, go, 0)
+        def go(other):
+            remote(row_out.at[k], row_in.at[k, p], sem_r_s.at[k], sem_r_r.at[k], other, y)
+
+        plane_peers(go)
 
     def row_finish(k):
         await_bytes(row_in.at[k, pl.ds(0, n_plane - 1)], sem_r_r.at[k])
@@ -235,20 +237,18 @@
             total = total + x[:, j * LANES : (j + 1) * LANES]
         return total
 
-    def scaled_fold(rows, mult):
+    def scaled_fold(rows):
         total = None
         for j in range(n_pt):
             x = e_ref[rows, j * LANES : (j + 1) * LANES]
-            if mult is not None:
-                x = x * mult[rows, j * LANES : (j + 1) * LANES]
             x = x * ubuf[j : j + 1, :]
             total = x if total is None else total + x
         return total
 
-    def row_pass(k, mult):
+    def row_pass(k):
         def go(i, c):
             rows = pl.ds(pl.multiple_of(i * chunk, chunk), chunk)
-            tcol[rows, :] = scaled_fold(rows, mult)
+            tcol[rows, :] = scaled_fold(rows)
             return c
 
         lax.fori_loop(0, crops // chunk, go, 0)
@@ -269,6 +269,8 @@
             col_out[k, j : j + 1, :] = jnp.sum(acc[j], axis=0, keepdims=True)
 
     gather_start(gt, 0)
+    w_copy.wait()
+    lax.fori_loop(0, protos // 256, prep_w, 0)
     for dx in groups:
         gather_group(gt, 0, dx)
         spread_group(gt, 0, dx)
@@ -276,37 +278,64 @@
     gather_finish(gt, 0)
     unit(gt, 0, TEACHER_TEMP, zt_cat, False)
 
+    wide = 1024
+
     def teacher_block(i, c):
-        cols = pl.ds(pl.multiple_of(i * 256, 256), 256)
+        cols = pl.ds(pl.multiple_of(i * wide, wide), wide)
         e = jnp.exp(nn(zt_cat[...], w_cat[:, cols]))
         e_ref[:, cols] = e
         sums = jnp.sum(e, axis=0, keepdims=True)
-        col_out[0, pl.ds(2 * i, 1), :] = sums[:, 0:LANES]
-        col_out[0, pl.ds(2 * i + 1, 1), :] = sums[:, LANES : 2 * LANES]
+        for j in range(wide // LANES):
+            col_out[0, pl.ds(wide // LANES * i + j, 1), :] = sums[:, j * LANES : (j + 1) * LANES]
         return c
 
-    lax.fori_loop(0, protos // 256, teacher_block, 0)
+    lax.fori_loop(0, protos // wide, teacher_block, 0)
     col_start(0)
     near_finish(gt, 0)
+    gather_group(gs, 1, 0)
     col_finish(0)
-    row_pass(0, None)
+    row_pass(0)
     row_start(0)
-    relay(gt, 0)
-
-    for dx in groups:
+
+    spread_group(gs, 1, 0)
+    for dx in groups[1:]:
         gather_group(gs, 1, dx)
-    spread_group(gs, 1, 0)
+        if dx != groups[3]:
+            spread_group(gs, 1, dx)
     gather_finish(gs, 1)
     unit(gs, 0, STUDENT_TEMP, zs_cat, True)
 
     def student_block(i, c):
-        cols = pl.ds(pl.multiple_of(i * 256, 256), 256)
+        cols = pl.ds(pl.multiple_of(i * wide, wide), wide)
         s = nn(zs_cat[...], w_cat[:, cols])
         s_log[:, cols] = s
         es_ref[:, cols] = jnp.exp(s)
         return c
 
-    lax.fori_loop(0, protos // 256, student_block, 0)
+    lax.fori_loop(0, protos // wide, student_block, 0)
+    def features_of(dst, scale_u):
+        def go(r, c):
+            rows = pl.ds(pl.multiple_of(r * 64, 64), 64)
+            cross = None
+            for j in range(n_pt):
+                lanes = slice(j * LANES, (j + 1) * LANES)
+                if scale_u:
+                    g = e_ref[rows, lanes] * ubuf[j : j + 1, :]
+                    term = g * s_log[rows, lanes]
+                    cross = term if cross is None else cross + term
+                else:
+                    g = es_ref[rows, lanes]
+                hi, lo = split(g)
+                g_hi[rows, lanes] = hi
+                g_lo[rows, lanes] = lo
+            if scale_u:
+                tcol[rows, :] = cross
+            return c
+
+        lax.fori_loop(0, crops // 64, go, 0)
+        w_hi, w_lo = w_cat[0:width, :], w_cat[2 * width : 3 * width, :]
+        dst[...] = nt(w_hi, g_hi[...]) + nt(w_hi, g_lo[...]) + nt(w_lo, g_hi[...])
+
     for k in (1, 2):
         to_column(1.0 / row_finish(k - 1))
         col_pass(k)
@@ -321,23 +350,23 @@
             to_rows(3)
             row_start(3)
             other_block(gt, 0, 1, TEACHER_TEMP, er, False)
+        else:
+            relay(gs, 1)
             far_finish(gt, 0)
-        else:
-            near_finish(gs, 1)
+            other_block(gs, 1, 1, STUDENT_TEMP, esr, True)
+            other_block(gs, 1, 3, STUDENT_TEMP, esr, True)
         col_finish(k)
-        row_pass(k, None)
+        row_pass(k)
         row_start(k)
         if k == 1:
-            for dx in groups[1:]:
-                spread_group(gs, 1, dx)
+            spread_group(gs, 1, groups[3])
+            relay(gt, 0)
             other_block(gt, 0, 3, TEACHER_TEMP, er, False)
-            other_block(gt, 0, 2, TEACHER_TEMP, er, False)
-        else:
-            relay(gs, 1)
-    row_pass(4, s_log)
-    row_start(4)
-    other_block(gs, 1, 1, STUDENT_TEMP, esr, True)
-    other_block(gs, 1, 3, STUDENT_TEMP, esr, True)
+            features_of(a1, False)
+            near_finish(gs, 1)
+    features_of(a2, True)
+    other_block(gt, 0, 2, TEACHER_TEMP, er, False)
+    far_finish(gs, 1)
     last = row_finish(2)
     student_total = row_finish(3)
     far[0, 0:n_ct, :] = scale / last
@@ -352,35 +381,60 @@
                 row = jnp.broadcast_to(far[rel, k : k + 1, :], (LANES, LANES))
                 dst[rows, :] = row.T
 
-    spread_columns(0, vcol, tcol)
-
-    def grad_block(r, c):
-        rows = pl.ds(pl.multiple_of(r * 32, 32), 32)
-        v = vcol[rows, :]
-        t = tcol[rows, :]
-        for j in range(n_pt):
-            lanes = slice(j * LANES, (j + 1) * LANES)
-            g = es_ref[rows, lanes] * t - e_ref[rows, lanes] * ubuf[j : j + 1, :] * v
-            hi, lo = split(g)
-            g_hi[rows, lanes] = hi
-            g_lo[rows, lanes] = lo
-        return c
-
-    lax.fori_loop(0, crops // 32, grad_block, 0)
-
-    gf_acc[...] = jnp.zeros_like(gf_acc)
-
-    def feat_block(i, c):
-        cols = pl.ds(pl.multiple_of(i * 512, 512), 512)
-        w_hi = w_cat[0:width, cols]
-        w_lo = w_cat[2 * width : 3 * width, cols]
-        gf_acc[...] += nt(w_hi, g_hi[:, cols]) + nt(w_hi, g_lo[:, cols]) + nt(w_lo, g_hi[:, cols])
-        return c
-
-    lax.fori_loop(0, protos // 512, feat_block, 0)
+    out_rows = width // n_y
+    half = 256
+
+    def rows_of(d):
+        return pl.ds(pl.multiple_of(d * out_rows, 8), out_rows)
+
+    def grads_of(rel, h):
+        def go(r, c):
+            rows = pl.ds(pl.multiple_of(r * 64, 64), 64)
+            v = vfar[rel, rows, :]
+            t = tfar[rel, rows, :]
+            for j in range(h * half // LANES, (h + 1) * half // LANES):
+                u = ubuf[pl.ds(y * (mine // LANES) + j, 1), :]
+                lanes = slice(j * LANES, (j + 1) * LANES)
+                if rel == 0:
+                    here = pl.ds(pl.multiple_of(y * mine + j * LANES, LANES), LANES)
+                    e, es = e_ref[rows, here], es_ref[rows, here]
+                else:
+                    e, es = er[rel - 1, rows, lanes], esr[rel - 1, rows, lanes]
+                hi, lo = split(es * t - e * u * v)
+                base = pl.multiple_of(rel * 3 * crops + r * 64, 64)
+                g_cat[pl.ds(base, 64), lanes] = hi
+                g_cat[pl.ds(base + crops, 64), lanes] = hi
+                g_cat[pl.ds(base + 2 * crops, 64), lanes] = lo
+            return c
+
+        lax.fori_loop(0, crops // 64, go, 0)
+
+    def proto_part(h):
+        part[h] = jnp.zeros((width, half), f32)
+
+        def go(q, c):
+            k = pl.ds(pl.multiple_of(q * 3 * crops, 3 * crops), 3 * crops)
+            part[h] += nn(z_cat[:, k], g_cat[k, h * half : (h + 1) * half])
+            return c
+
+        lax.fori_loop(0, n_y, go, 0)
+        final[h, pl.ds(y, 1)] = part[h, rows_of(y)][None]
+        for i in (2, 1, 3):
+            to = lax.rem(y + i, n_y)
+            remote(part.at[h, rows_of(to)], final.at[h, y], sem_y_s.at[h], sem_y_r.at[h], p, to)
+
+    spread_columns(0, vfar.at[0], tfar.at[0])
+
+    cross = jnp.sum(tcol[...] * vfar[0], axis=0, keepdims=True)
+    lse = jnp.sum(jnp.log(student_total), axis=0, keepdims=True)
     for ct in range(n_ct):
-        rs_flat[pl.ds(ct, width, stride=n_ct), :] = gf_acc[:, ct * LANES : (ct + 1) * LANES]
-    rs_src[...] = rs_flat[...].reshape(rs_src.shape)
+        lanes = slice(ct * LANES, (ct + 1) * LANES)
+        t, v = far[0, n_ct + ct : n_ct + ct + 1, :], far[0, ct : ct + 1, :]
+        rs_flat[pl.ds(ct, width, stride=n_ct), :] = a1[:, lanes] * t - a2[:, lanes] * v
+    slab = feat * n_ct
+    rs_src[:, :, 0:slab, :] = rs_flat[...].reshape((n_chip, 2, slab, LANES))
+    loss_row = lse * (1.0 / n_plane) - cross * (1.0 / scale)
+    rs_src[:, :, slab : slab + 1, :] = jnp.broadcast_to(loss_row, (n_chip, 2, 1, LANES))
     pair = pltpu.make_async_remote_copy(
         src_ref=rs_src.at[:, 1 - core],
         dst_ref=rs_pair,
@@ -390,11 +444,9 @@
         device_id_type=MESH,
     )
     pair.start()
-    cross = row_finish(4)
-    loss_in[pl.ds(y, 1)] = (jnp.log(student_total) - cross / last)[None]
-    for i in range(1, n_y):
-        remote(loss_in.at[y], loss_in.at[y], sem_l_s.at[0], sem_l_r.at[0], p, lax.rem(y + i, n_y))
-    far_finish(gs, 1)
+    for h in range(mine // 256):
+        grads_of(0, h)
+    other_block(gs, 1, 2, STUDENT_TEMP, esr, True)
     pair.wait()
     rs_pair[...] += rs_src[:, core]
     rs_in[pl.ds(chip, 1)] = rs_pair[pl.ds(chip, 1)]
@@ -412,55 +464,19 @@
         return c
 
     lax.fori_loop(1, n_chip, scatter, 0)
-    other_block(gs, 1, 2, STUDENT_TEMP, esr, True)
     await_bytes(far.at[pl.ds(1, n_y - 1)], sem_v_r.at[0])
     for rel in range(1, n_y):
-        spread_columns(rel, vfar.at[rel - 1], tfar.at[rel - 1])
-
-    out_rows = width // n_y
-    half = 256
-
-    def rows_of(d):
-        return pl.ds(pl.multiple_of(d * out_rows, 8), out_rows)
-
-    def proto_part(h):
-        base = pl.multiple_of(y * mine + h * half, half)
-        lanes_r = slice(h * half, (h + 1) * half)
-        own = pl.ds(base, half)
+        spread_columns(rel, vfar.at[rel], tfar.at[rel])
+    for h in range(mine // half):
         for rel in range(1, n_y):
-            def go(r, c):
-                rows = pl.ds(pl.multiple_of(r * 64, 64), 64)
-                v = vfar[rel - 1, rows, :]
-                t = tfar[rel - 1, rows, :]
-                for j in range(half // LANES):
-                    lanes = slice(h * half + j * LANES, h * half + (j + 1) * LANES)
-                    u = ubuf[pl.ds(y * (mine // LANES) + h * (half // LANES) + j, 1), :]
-                    g = esr[rel - 1, rows, lanes] * t - er[rel - 1, rows, lanes] * u * v
-                    hi, lo = split(g)
-                    gr_hi[rel - 1, rows, lanes] = hi
-                    gr_lo[rel - 1, rows, lanes] = lo
-                return c
-
-            lax.fori_loop(0, crops // 64, go, 0)
-        total = None
-        for rel in range(n_y):
-            if rel == 0:
-                a, b = g_hi[:, own], g_lo[:, own]
-            else:
-                a, b = gr_hi[rel - 1, :, lanes_r], gr_lo[rel - 1, :, lanes_r]
-            piece = nn(zs_hi[rel], a) + nn(zs_lo[rel], a) + nn(zs_hi[rel], b)
-            total = piece if total is None else total + piece
-        part[h] = total
-        final[h, pl.ds(y, 1)] = part[h, rows_of(y)][None]
-        for i in range(1, n_y):
-            to = lax.rem(y + i, n_y)
-            remote(part.at[h, rows_of(to)], final.at[h, y], sem_y_s.at[h], sem_y_r.at[h], p, to)
-
-    for h in range(mine // half):
+            grads_of(rel, h)
         proto_part(h)
 
     await_bytes(rs_in.at[pl.ds(0, n_chip - 1)], sem_f_r.at[1])
     total = jnp.sum(rs_in[...], axis=0)
+    loss_in[pl.ds(y, 1)] = total[slab : slab + 1, :][None]
+    for i in range(1, n_y):
+        remote(loss_in.at[y], loss_in.at[y], sem_l_s.at[0], sem_l_r.at[0], p, lax.rem(y + i, n_y))
     for j in range(feat):
         for ct in range(n_ct):
             k = n_ct * j + ct
@@ -473,7 +489,8 @@
     loss_ref[0, 0] = jnp.sum(jnp.sum(loss_in[...], axis=0)) * (1.0 / crops_all)
 
     for k, buf in ((0, gt), (1, gs)):
-        await_bytes(buf.at[0, pl.ds(0, n_chip - 1), core], sem_g_s.at[k])
+        await_bytes(buf.at[0, pl.ds(0, 2 * n_z - 1), core], sem_g_s.at[k])
+        await_bytes(buf.at[0, pl.ds(0, 2 * n_z), core], sem_x_s.at[k])
         await_bytes(buf.at[0, :, core], sem_d_s.at[k])
         for i in range(2):
             await_bytes(buf.at[0, :, core], sem_a_s.at[k, i])
@@ -487,7 +504,7 @@
     await_bytes(rs_in.at[pl.ds(0, n_chip - 1)], sem_f_s.at[1])
     for k in range(3):
         await_bytes(col_in.at[k, pl.ds(0, n_y - 1)], sem_c_s.at[k])
-    for k in range(5):
+    for k in range(4):
         await_bytes(row_in.at[k, pl.ds(0, n_plane - 1)], sem_r_s.at[k])
 
 
@@ -525,8 +542,7 @@
             vm((width * n_ct, LANES), f32),
             vm((crops, 3 * width), bf16),
             vm((crops, 3 * width), bf16),
-            vm((n_y, width, crops), bf16),
-            vm((n_y, width, crops), bf16),
+            vm((width, 3 * n_y * crops), bf16),
             vm((3 * width, protos), bf16),
             vm((crops, protos), f32),
             vm((crops, protos), f32),
@@ -535,31 +551,30 @@
             vm((crops, protos), bf16),
             vm((n_y - 1, crops, mine), f32),
             vm((n_y - 1, crops, mine), f32),
-            vm((n_y - 1, crops, mine), bf16),
-            vm((n_y - 1, crops, mine), bf16),
+            vm((3 * n_y * crops, mine), bf16),
             vm((n_y, 2 * n_ct, LANES), f32),
-            vm((n_y - 1, crops, LANES), f32),
-            vm((n_y - 1, crops, LANES), f32),
+            vm((n_y, crops, LANES), f32),
+            vm((n_y, crops, LANES), f32),
+            vm((width, crops), f32),
+            vm((width, crops), f32),
             vm((crops, LANES), f32),
             vm((crops, LANES), f32),
             vm((3, n_pt, LANES), f32),
             vm((3, n_y, n_pt, LANES), f32),
             vm((n_pt, LANES), f32),
-            vm((5, n_ct, LANES), f32),
-            vm((5, n_plane, n_ct, LANES), f32),
-            vm((width, crops), f32),
+            vm((4, n_ct, LANES), f32),
+            vm((4, n_plane, n_ct, LANES), f32),
             vm((width * n_ct, LANES), f32),
-            vm(slots, f32),
-            vm((n_chip, feat * n_ct, LANES), f32),
-            vm((n_chip, feat * n_ct, LANES), f32),
-            vm((n_y, n_ct, LANES), f32),
-            vm((width, protos), f32),
+            vm((n_chip, 2, feat * n_ct + 1, LANES), f32),
+            vm((n_chip, feat * n_ct + 1, LANES), f32),
+            vm((n_chip, feat * n_ct + 1, LANES), f32),
+            vm((n_y, 1, LANES), f32),
             vm((mine // 256, width, 256), f32),
             vm((mine // 256, n_y, width // n_y, 256), f32),
-            dma((2,)), dma((2, 4)), dma((2,)), dma((2,)), dma((3,)), dma((3,)), dma((5,)), dma((5,)),
+            dma((2,)), dma((2, 4)), dma((2,)), dma((2,)), dma((3,)), dma((3,)), dma((4,)), dma((4,)),
             dma((2,)), dma((2,)), dma((1,)), dma((1,)),
             dma((1,)), dma((mine // 256,)), dma((mine // 256,)), dma((2, 4)), dma((2, 4)),
-            dma((2, 3)), dma((2, 3)), dma((1,)), dma((1,)),
+            dma((2, 3)), dma((2, 3)), dma((1,)), dma((1,)), dma((2,)),
         ],
         compiler_params=pltpu.CompilerParams(
             collective_id=0, has_side_effects=True, vmem_limit_bytes=60 * 2**20

time: 97.2 us -> 88.3 us (0.908)
  Pallas kernels: 91 us -> 82.1 us
    pallas_call x1, Pallas kernels: 91 us -> 82.1 us  [on_device(): pl.pallas_call(functools.partial(kernel, n_y, n_chip, scale, crops * n_y)...]
where the time goes in v4:
time: 88.3 us; the launch traced here: 87.9 us
  Pallas kernels  82.1 us (93%)
  local copies, waits for them, and re-layouts  3.39 us (4%)
  between operations  2.41 us (3%)
    pallas_call x1, Pallas kernels, on_device(): pl.pallas_call(functools.partial(kernel, n_y, n_chip, scale, crops * n_y)...  82.1 us
    unnamed x2, local copies, waits for them, and re-layouts  3.39 us

profile of v4, /device:TPU:1, one launch (start us, length us, event | category | flops | bytes accessed | tf_op | source)
XLA Modules:
  0.0 87.9 jit_solution(16591824906274064106)
XLA Ops:
  0.6 82.1 %shard_map.58 = (f32[6,512]{1,0:T(8,128)}, f32[96,2048]{1,0:T(8,128)}, f32[1,1]{1,0:T(1,128)}) custom-call(f32[6,512]{1,0:T(8,128)} %t_ref.1, f32[6,512]{1,0:T(8,128)} %s_ref.1, f32[384,2048]{1,0:T(8,128)} %w_ref.1), custom_call_target="tpu_custom_call" | custom-call | tf_op jit(solution)/shard_map/pallas_call | solution.py:522
  82.7 1.3 %copy.9 = f32[6,512]{1,0:T(8,128)} copy(f32[6,512]{1,0:T(8,128)} %get-tuple-element.12) | data formatting | bytes 24576
  84.1 2.1 %copy.10 = f32[96,2048]{1,0:T(8,128)} copy(f32[96,2048]{1,0:T(8,128)} %get-tuple-element.13) | data formatting | bytes 1572864

commit v5 on v4

--- a/solution.py
+++ b/solution.py
@@ -42,7 +42,7 @@
     gt, gs, flat, zt_cat, zs_cat, z_cat, w_cat, e_ref, s_log, es_ref, g_hi, g_lo,
     er, esr, g_cat, far, vfar, tfar, a1, a2,
     tcol, vcol, col_out, col_in, ubuf, row_out, row_in, rs_flat, rs_src, rs_pair, rs_in,
-    loss_in, part, final,
+    loss_in, loss_sum, part, final, t_raw, s_raw,
     sem_g_s, sem_g_r, sem_d_s, sem_d_r, sem_c_s, sem_c_r, sem_r_s, sem_r_r, sem_f_s, sem_f_r,
     sem_l_s, sem_l_r, sem_w, sem_y_s, sem_y_r, sem_a_s, sem_a_r,
     sem_e_s, sem_e_r, sem_v_s, sem_v_r, sem_x_s,
@@ -53,7 +53,11 @@
     core = p % 2
     width, protos = w_ref.shape
     w_raw = s_log.at[0:width]
+    t_copy = pltpu.make_async_copy(t_ref, t_raw, sem_w.at[1])
+    s_copy = pltpu.make_async_copy(s_ref, s_raw, sem_w.at[2])
     w_copy = pltpu.make_async_copy(w_ref, w_raw, sem_w.at[0])
+    t_copy.start()
+    s_copy.start()
     w_copy.start()
     crops = e_ref.shape[0]
     n_ct = crops // LANES
@@ -86,9 +90,12 @@
 
     plane_peers(greet)
     for i in range(1, n_y):
-        pl.semaphore_signal(bar, inc=1, device_id=(p, lax.rem(y + i, n_y)), device_id_type=MESH)
-
-    for src, dst in ((t_ref, gt), (s_ref, gs)):
+        for to in (p, sibling):
+            pl.semaphore_signal(bar, inc=1, device_id=(to, lax.rem(y + i, n_y)), device_id_type=MESH)
+
+    t_copy.wait()
+    s_copy.wait()
+    for src, dst in ((t_raw, gt), (s_raw, gs)):
         for j in range(feat):
             for ct in range(n_ct):
                 k = n_ct * j + ct
@@ -104,7 +111,7 @@
         w_cat[2 * width : 3 * width, cols] = lo
         return c
 
-    pl.semaphore_wait(bar, n_plane - 1 + n_y - 1)
+    pl.semaphore_wait(bar, n_plane - 1 + 2 * (n_y - 1))
 
     def remote(src, dst, s, r, plane, crop):
         copy = pltpu.make_async_remote_copy(
@@ -291,12 +298,11 @@
 
     lax.fori_loop(0, protos // wide, teacher_block, 0)
     col_start(0)
+    gather_group(gs, 1, 0)
     near_finish(gt, 0)
-    gather_group(gs, 1, 0)
     col_finish(0)
     row_pass(0)
     row_start(0)
-
     spread_group(gs, 1, 0)
     for dx in groups[1:]:
         gather_group(gs, 1, dx)
@@ -341,6 +347,8 @@
         col_pass(k)
         col_start(k)
         if k == 1:
+            relay(gt, 0)
+
             def fold(i, c):
                 rows = pl.ds(pl.multiple_of(i * chunk, chunk), chunk)
                 tcol[rows, :] = lane_fold(es_ref[rows, :])
@@ -352,20 +360,19 @@
             other_block(gt, 0, 1, TEACHER_TEMP, er, False)
         else:
             relay(gs, 1)
-            far_finish(gt, 0)
+            other_block(gt, 0, 2, TEACHER_TEMP, er, False)
             other_block(gs, 1, 1, STUDENT_TEMP, esr, True)
-            other_block(gs, 1, 3, STUDENT_TEMP, esr, True)
         col_finish(k)
         row_pass(k)
         row_start(k)
         if k == 1:
             spread_group(gs, 1, groups[3])
-            relay(gt, 0)
             other_block(gt, 0, 3, TEACHER_TEMP, er, False)
             features_of(a1, False)
+            far_finish(gt, 0)
             near_finish(gs, 1)
     features_of(a2, True)
-    other_block(gt, 0, 2, TEACHER_TEMP, er, False)
+    other_block(gs, 1, 3, STUDENT_TEMP, esr, True)
     far_finish(gs, 1)
     last = row_finish(2)
     student_total = row_finish(3)
@@ -382,59 +389,60 @@
                 dst[rows, :] = row.T
 
     out_rows = width // n_y
-    half = 256
+    half = LANES
 
     def rows_of(d):
         return pl.ds(pl.multiple_of(d * out_rows, 8), out_rows)
 
-    def grads_of(rel, h):
+    def grads_of(rel, c0):
+        lanes = pl.ds(pl.multiple_of(c0 * LANES, LANES), LANES)
+        here = pl.ds(pl.multiple_of(y * mine + c0 * LANES, LANES), LANES)
+        u = ubuf[pl.ds(y * (mine // LANES) + c0, 1), :]
+
         def go(r, c):
             rows = pl.ds(pl.multiple_of(r * 64, 64), 64)
             v = vfar[rel, rows, :]
             t = tfar[rel, rows, :]
-            for j in range(h * half // LANES, (h + 1) * half // LANES):
-                u = ubuf[pl.ds(y * (mine // LANES) + j, 1), :]
-                lanes = slice(j * LANES, (j + 1) * LANES)
-                if rel == 0:
-                    here = pl.ds(pl.multiple_of(y * mine + j * LANES, LANES), LANES)
-                    e, es = e_ref[rows, here], es_ref[rows, here]
-                else:
-                    e, es = er[rel - 1, rows, lanes], esr[rel - 1, rows, lanes]
-                hi, lo = split(es * t - e * u * v)
-                base = pl.multiple_of(rel * 3 * crops + r * 64, 64)
-                g_cat[pl.ds(base, 64), lanes] = hi
-                g_cat[pl.ds(base + crops, 64), lanes] = hi
-                g_cat[pl.ds(base + 2 * crops, 64), lanes] = lo
+            if rel == 0:
+                e, es = e_ref[rows, here], es_ref[rows, here]
+            else:
+                e, es = er[rel - 1, rows, lanes], esr[rel - 1, rows, lanes]
+            hi, lo = split(es * t - e * u * v)
+            base = pl.multiple_of(rel * 3 * crops + r * 64, 64)
+            g_cat[pl.ds(base, 64), lanes] = hi
+            g_cat[pl.ds(base + crops, 64), lanes] = hi
+            g_cat[pl.ds(base + 2 * crops, 64), lanes] = lo
             return c
 
         lax.fori_loop(0, crops // 64, go, 0)
 
-    def proto_part(h):
-        part[h] = jnp.zeros((width, half), f32)
-
-        def go(q, c):
-            k = pl.ds(pl.multiple_of(q * 3 * crops, 3 * crops), 3 * crops)
-            part[h] += nn(z_cat[:, k], g_cat[k, h * half : (h + 1) * half])
-            return c
-
-        lax.fori_loop(0, n_y, go, 0)
+    def proto_part(h, carry):
+        for rel in range(1, n_y):
+            grads_of(rel, h)
+        lanes = pl.ds(pl.multiple_of(h * half, half), half)
+        part[h] = nn(z_cat[...], g_cat[:, lanes])
         final[h, pl.ds(y, 1)] = part[h, rows_of(y)][None]
         for i in (2, 1, 3):
             to = lax.rem(y + i, n_y)
             remote(part.at[h, rows_of(to)], final.at[h, y], sem_y_s.at[h], sem_y_r.at[h], p, to)
+        return carry
 
     spread_columns(0, vfar.at[0], tfar.at[0])
 
     cross = jnp.sum(tcol[...] * vfar[0], axis=0, keepdims=True)
     lse = jnp.sum(jnp.log(student_total), axis=0, keepdims=True)
+    loss_in[pl.ds(2 * y + core, 1)] = (lse * (1.0 / n_plane) - cross * (1.0 / scale))[None]
+    for i in range(n_y):
+        for c in range(2):
+            if i or c:
+                here = loss_in.at[2 * y + core]
+                to = 2 * chip + lax.rem(core + c, 2)
+                remote(here, here, sem_l_s.at[0], sem_l_r.at[0], to, lax.rem(y + i, n_y))
     for ct in range(n_ct):
         lanes = slice(ct * LANES, (ct + 1) * LANES)
         t, v = far[0, n_ct + ct : n_ct + ct + 1, :], far[0, ct : ct + 1, :]
         rs_flat[pl.ds(ct, width, stride=n_ct), :] = a1[:, lanes] * t - a2[:, lanes] * v
-    slab = feat * n_ct
-    rs_src[:, :, 0:slab, :] = rs_flat[...].reshape((n_chip, 2, slab, LANES))
-    loss_row = lse * (1.0 / n_plane) - cross * (1.0 / scale)
-    rs_src[:, :, slab : slab + 1, :] = jnp.broadcast_to(loss_row, (n_chip, 2, 1, LANES))
+    rs_src[...] = rs_flat[...].reshape(rs_src.shape)
     pair = pltpu.make_async_remote_copy(
         src_ref=rs_src.at[:, 1 - core],
         dst_ref=rs_pair,
@@ -444,9 +452,7 @@
         device_id_type=MESH,
     )
     pair.start()
-    for h in range(mine // 256):
-        grads_of(0, h)
-    other_block(gs, 1, 2, STUDENT_TEMP, esr, True)
+    lax.fori_loop(0, mine // half, lambda h, c: (grads_of(0, h), c)[1], 0)
     pair.wait()
     rs_pair[...] += rs_src[:, core]
     rs_in[pl.ds(chip, 1)] = rs_pair[pl.ds(chip, 1)]
@@ -464,19 +470,23 @@
         return c
 
     lax.fori_loop(1, n_chip, scatter, 0)
+    other_block(gs, 1, 2, STUDENT_TEMP, esr, True)
     await_bytes(far.at[pl.ds(1, n_y - 1)], sem_v_r.at[0])
     for rel in range(1, n_y):
         spread_columns(rel, vfar.at[rel], tfar.at[rel])
-    for h in range(mine // half):
-        for rel in range(1, n_y):
-            grads_of(rel, h)
-        proto_part(h)
+    lax.fori_loop(0, mine // half, proto_part, 0)
+    await_bytes(loss_in.at[pl.ds(0, 2 * n_y - 1)], sem_l_r.at[0])
+    loss_sum[pl.ds(chip, 1)] = jnp.sum(loss_in[...], axis=0, keepdims=True)
+
+    def scatter_loss(i, c):
+        here = loss_sum.at[chip]
+        remote(here, here, sem_l_s.at[1], sem_l_r.at[1], lax.rem(chip + i, n_chip) * 2 + core, y)
+        return c
+
+    lax.fori_loop(1, n_chip, scatter_loss, 0)
 
     await_bytes(rs_in.at[pl.ds(0, n_chip - 1)], sem_f_r.at[1])
     total = jnp.sum(rs_in[...], axis=0)
-    loss_in[pl.ds(y, 1)] = total[slab : slab + 1, :][None]
-    for i in range(1, n_y):
-        remote(loss_in.at[y], loss_in.at[y], sem_l_s.at[0], sem_l_r.at[0], p, lax.rem(y + i, n_y))
     for j in range(feat):
         for ct in range(n_ct):
             k = n_ct * j + ct
@@ -485,8 +495,8 @@
         await_bytes(final.at[h, pl.ds(0, n_y - 1)], sem_y_r.at[h])
         for q in range(n_y):
             gp_ref[:, q * mine + h * half : q * mine + (h + 1) * half] = final[h, q]
-    await_bytes(loss_in.at[pl.ds(0, n_y - 1)], sem_l_r.at[0])
-    loss_ref[0, 0] = jnp.sum(jnp.sum(loss_in[...], axis=0)) * (1.0 / crops_all)
+    await_bytes(loss_sum.at[pl.ds(0, n_chip - 1)], sem_l_r.at[1])
+    loss_ref[0, 0] = jnp.sum(jnp.sum(loss_sum[...], axis=0)) * (1.0 / crops_all)
 
     for k, buf in ((0, gt), (1, gs)):
         await_bytes(buf.at[0, pl.ds(0, 2 * n_z - 1), core], sem_g_s.at[k])
@@ -500,7 +510,8 @@
     await_bytes(far.at[pl.ds(1, n_y - 1)], sem_v_s.at[0])
     for h in range(mine // half):
         await_bytes(final.at[h, pl.ds(0, n_y - 1)], sem_y_s.at[h])
-    await_bytes(loss_in.at[pl.ds(0, n_y - 1)], sem_l_s.at[0])
+    await_bytes(loss_in.at[pl.ds(0, 2 * n_y - 1)], sem_l_s.at[0])
+    await_bytes(loss_sum.at[pl.ds(0, n_chip - 1)], sem_l_s.at[1])
     await_bytes(rs_in.at[pl.ds(0, n_chip - 1)], sem_f_s.at[1])
     for k in range(3):
         await_bytes(col_in.at[k, pl.ds(0, n_y - 1)], sem_c_s.at[k])
@@ -522,13 +533,13 @@
     gf, gp, loss = pl.pallas_call(
         functools.partial(kernel, n_y, n_chip, scale, crops * n_y),
         out_shape=(
-            jax.ShapeDtypeStruct((feat, crops), f32),
-            jax.ShapeDtypeStruct((width // n_y, protos), f32),
+            pltpu.VMEM((feat, crops), f32),
+            pltpu.VMEM((width // n_y, protos), f32),
             jax.ShapeDtypeStruct((1, 1), f32),
         ),
         in_specs=[
-            pl.BlockSpec(memory_space=vm),
-            pl.BlockSpec(memory_space=vm),
+            pl.BlockSpec(memory_space=pl.ANY),
+            pl.BlockSpec(memory_space=pl.ANY),
             pl.BlockSpec(memory_space=pl.ANY),
         ],
         out_specs=(
@@ -565,15 +576,18 @@
             vm((4, n_ct, LANES), f32),
             vm((4, n_plane, n_ct, LANES), f32),
             vm((width * n_ct, LANES), f32),
-            vm((n_chip, 2, feat * n_ct + 1, LANES), f32),
-            vm((n_chip, feat * n_ct + 1, LANES), f32),
-            vm((n_chip, feat * n_ct + 1, LANES), f32),
-            vm((n_y, 1, LANES), f32),
-            vm((mine // 256, width, 256), f32),
-            vm((mine // 256, n_y, width // n_y, 256), f32),
+            vm(slots, f32),
+            vm(slots[:1] + slots[2:], f32),
+            vm(slots[:1] + slots[2:], f32),
+            vm((2 * n_y, 1, LANES), f32),
+            vm((n_chip, 1, LANES), f32),
+            vm((mine // 128, width, 128), f32),
+            vm((mine // 128, n_y, width // n_y, 128), f32),
+            vm((feat, crops), f32),
+            vm((feat, crops), f32),
             dma((2,)), dma((2, 4)), dma((2,)), dma((2,)), dma((3,)), dma((3,)), dma((4,)), dma((4,)),
-            dma((2,)), dma((2,)), dma((1,)), dma((1,)),
-            dma((1,)), dma((mine // 256,)), dma((mine // 256,)), dma((2, 4)), dma((2, 4)),
+            dma((2,)), dma((2,)), dma((2,)), dma((2,)),
+            dma((3,)), dma((mine // 128,)), dma((mine // 128,)), dma((2, 4)), dma((2, 4)),
             dma((2, 3)), dma((2, 3)), dma((1,)), dma((1,)), dma((2,)),
         ],
         compiler_params=pltpu.CompilerParams(

time: 88.3 us -> 83.4 us (0.945)
  Pallas kernels: 82.1 us -> 79.5 us
  local copies, waits for them, and re-layouts: 3.39 us -> 1.49 us
    pallas_call x1, Pallas kernels: 82.1 us -> 79.5 us  [on_device(): pl.pallas_call(functools.partial(kernel, n_y, n_chip, scale, crops * n_y)...]
    unnamed x2, local copies, waits for them, and re-layouts: 3.39 us -> 1.49 us
where the time goes in v5:
time: 83.4 us; the launch traced here: 83.3 us
  Pallas kernels  79.5 us (95%)
  between operations  2.33 us (3%)
  local copies, waits for them, and re-layouts  1.49 us (2%)
    pallas_call x1, Pallas kernels, on_device(): pl.pallas_call(functools.partial(kernel, n_y, n_chip, scale, crops * n_y)...  79.5 us

profile of v5, /device:TPU:1, one launch (start us, length us, event | category | flops | bytes accessed | tf_op | source)
XLA Modules:
  0.0 83.3 jit_solution(8635414031717829341)
XLA Ops:
  0.6 79.5 %shard_map.58 = (f32[6,512]{1,0:T(8,128)S(1)}, f32[96,2048]{1,0:T(8,128)S(1)}, f32[1,1]{1,0:T(1,128)}) custom-call(f32[6,512]{1,0:T(8,128)} %t_ref.1, f32[6,512]{1,0:T(8,128)} %s_ref.1, f32[384,2048]{1,0:T(8,128)} %w_ref.1), custom_call_target="tpu_custom_call" | custom-call | tf_op jit(solution)/shard_map/pallas_call | solution.py:533
  80.1 0.6 copy.9
  80.7 0.9 %copy.10 = f32[96,2048]{1,0:T(8,128)} copy(f32[96,2048]{1,0:T(8,128)S(1)} %get-tuple-element.10) | data formatting | bytes 1572864

commit v6 on v5

--- a/solution.py
+++ b/solution.py
@@ -78,12 +78,18 @@
     bar = pltpu.get_barrier_semaphore()
 
     def plane_peers(go):
-        def step(i, c):
-            go(lax.rem(p + i, n_plane))
-            return c
-
-        lax.fori_loop(24, n_plane, step, 0)
-        lax.fori_loop(1, 24, step, 0)
+        def four(base):
+            def step(i, c):
+                for j in range(4):
+                    go(lax.rem(p + base + 4 * i + j, n_plane))
+                return c
+
+            return step
+
+        lax.fori_loop(0, (n_plane - 24) // 4, four(24), 0)
+        lax.fori_loop(0, 5, four(1), 0)
+        for k in range(21, 24):
+            go(lax.rem(p + k, n_plane))
 
     def greet(other):
         pl.semaphore_signal(bar, inc=1, device_id=(other, y), device_id_type=MESH)
@@ -372,8 +378,9 @@
             far_finish(gt, 0)
             near_finish(gs, 1)
     features_of(a2, True)
+    far_finish(gs, 1)
     other_block(gs, 1, 3, STUDENT_TEMP, esr, True)
-    far_finish(gs, 1)
+    other_block(gs, 1, 2, STUDENT_TEMP, esr, True)
     last = row_finish(2)
     student_total = row_finish(3)
     far[0, 0:n_ct, :] = scale / last
@@ -470,7 +477,6 @@
         return c
 
     lax.fori_loop(1, n_chip, scatter, 0)
-    other_block(gs, 1, 2, STUDENT_TEMP, esr, True)
     await_bytes(far.at[pl.ds(1, n_y - 1)], sem_v_r.at[0])
     for rel in range(1, n_y):
         spread_columns(rel, vfar.at[rel], tfar.at[rel])

time: 83.4 us -> 82.8 us (level)
  no operation moved by 1% of the time
where the time goes in v6:
time: 82.8 us; the launch traced here: 82.7 us
  Pallas kernels  78.9 us (95%)
  between operations  2.33 us (3%)
  local copies, waits for them, and re-layouts  1.49 us (2%)
    pallas_call x1, Pallas kernels, on_device(): pl.pallas_call(functools.partial(kernel, n_y, n_chip, scale, crops * n_y)...  78.9 us

profile of v6, /device:TPU:1, one launch (start us, length us, event | category | flops | bytes accessed | tf_op | source)
XLA Modules:
  0.0 82.7 jit_solution(8212791529621137832)
XLA Ops:
  0.6 78.9 %shard_map.58 = (f32[6,512]{1,0:T(8,128)S(1)}, f32[96,2048]{1,0:T(8,128)S(1)}, f32[1,1]{1,0:T(1,128)}) custom-call(f32[6,512]{1,0:T(8,128)} %t_ref.1, f32[6,512]{1,0:T(8,128)} %s_ref.1, f32[384,2048]{1,0:T(8,128)} %w_ref.1), custom_call_target="tpu_custom_call" | custom-call | tf_op jit(solution)/shard_map/pallas_call | solution.py:539
  79.5 0.6 copy.9
  80.1 0.9 %copy.10 = f32[96,2048]{1,0:T(8,128)} copy(f32[96,2048]{1,0:T(8,128)S(1)} %get-tuple-element.10) | data formatting | bytes 1572864
